TPU v7x, 256 devices: a whole 4x4x8 slice. The times are simulated.
256 devices in a mesh: tm: 64 (over z, y, core), rec: 4 (over x).
Axes of the slice: x: 4, y: 4, z: 8, core: 2. Of those that a mesh axis runs over, the one named last changes fastest.
Arguments:
- activations: bfloat16 [8, 16384, 512], P('rec', 'tm'), may hold values from -16 to 16
- cotangent: bfloat16 [8, 16384, 512], P('rec', 'tm'), may hold values from -6 to 6
- retain: float32 [8, 16384], P('rec', 'tm'), may hold values from 0.5 to 1
- dilation: int32 [9], replicated, may hold values from 0 to 128, as said below
- conv_w: float32 [9, 512], replicated, may hold values from -2 to 2
- skip_gain: float32 [512], replicated, may hold values from -6 to 6
- log_rate: float32 [512], replicated
- mode_angle: float32 [512], replicated, may hold values from -3.140625 to 3.140625
- w_in: bfloat16 [512, 1024], replicated, may hold values from -0.25 to 0.25
- w_out: bfloat16 [1024, 512], replicated, may hold values from -0.1875 to 0.1875
Outputs:
- grad_input: bfloat16 [8, 16384, 512], P('rec', 'tm')
- grad_taps: float32 [9, 512], replicated
- grad_skip: float32 [512], replicated
- grad_log_rate: float32 [512], replicated
- grad_angle: float32 [512], replicated
- grad_w_in: float32 [512, 1024], P('tm')
- grad_w_out: float32 [1024, 512], P('tm')
Inputs may be any that keep to these rules, and one draw needn't show every extreme that they name: dilation[0] is 0, dilation[8] is 128, and the lags rise strictly.
All inputs are finite; a program needn't handle non-finite values.
Results may differ from a plain program's by a relative error of at most 0.01235.
Values may be sent and summed in bfloat16 or wider, within the bound.
A program may use at most 64 MiB of HBM per device.

v0:
```python
import math

import jax
import jax.numpy as jnp
from jax import lax
from jax.sharding import PartitionSpec as P

TAPS = 9
MAXLAG = 128


block_span = 16


def from_behind(x, axis, by):
    size = lax.axis_size(axis)
    pairs = [(i, i + by) for i in range(size) if 0 <= i + by < size]
    return lax.ppermute(x, axis, pairs)


def entering(part, axis, combine, identity, reverse):
    count = lax.axis_size(axis)
    place = lax.axis_index(axis)
    ahead = count - 1 - place if reverse else place
    gathered = jax.tree.map(lambda a: lax.all_gather(a, axis), part)
    state = jax.tree.map(lambda a, e: jnp.zeros_like(a) + jnp.asarray(e, a.dtype), part, identity)

    def one(hop, state):
        source = count - 1 - hop if reverse else hop
        return combine(
            state, jax.tree.map(lambda a: lax.dynamic_index_in_dim(a, source, 0, False), gathered)
        )

    return lax.fori_loop(0, ahead, one, state)


def complex_mul(left_re, left_im, right_re, right_im):
    return (left_re * right_re - left_im * right_im, left_re * right_im + left_im * right_re)


def compose(earlier, later):
    early_pre, early_pim, early_bre, early_bim = earlier
    late_pre, late_pim, late_bre, late_bim = later
    prod_re, prod_im = complex_mul(late_pre, late_pim, early_pre, early_pim)
    moved_re, moved_im = complex_mul(late_pre, late_pim, early_bre, early_bim)
    return (prod_re, prod_im, moved_re + late_bre, moved_im + late_bim)


def decay_params(log_rate, mode_angle):
    decay_rate = jnp.exp(log_rate)
    radius = jnp.exp(-decay_rate)
    lam_re = radius * jnp.cos(mode_angle)
    lam_im = radius * jnp.sin(mode_angle)
    in_gain = jnp.sqrt(-jnp.expm1(-2.0 * decay_rate))
    return (decay_rate, radius, lam_re, lam_im, in_gain)


def lam_power(decay_rate, mode_angle, exponent, conj_sign):
    magnitude = jnp.exp(-exponent[:, None] * decay_rate[None, :])
    phase = exponent[:, None] * mode_angle[None, :]
    return (magnitude * jnp.cos(phase), conj_sign * magnitude * jnp.sin(phase))


def local_sweep(vals_re, vals_im, keep_tile, decay_rate, mode_angle, lam_re, lam_im, backward):
    block_len = vals_re.shape[0]
    conj_sign = -1.0 if backward else 1.0
    turn_im = conj_sign * lam_im

    def advance_back(state_pair, step_in):
        pre_re, pre_im = state_pair
        value_re, value_im, keep_step = step_in
        new_re = value_re + pre_re
        new_im = value_im + pre_im
        rot_re, rot_im = complex_mul(lam_re, turn_im, new_re, new_im)
        factor = keep_step[..., None]
        return ((factor * rot_re, factor * rot_im), (new_re, new_im))

    def advance_fwd(state_pair, step_in):
        old_re, old_im = state_pair
        value_re, value_im, keep_step = step_in
        rot_re, rot_im = complex_mul(lam_re, turn_im, old_re, old_im)
        factor = keep_step[..., None]
        new_re = factor * rot_re + value_re
        new_im = factor * rot_im + value_im
        return ((new_re, new_im), (new_re, new_im))

    zeros_state = jnp.zeros(vals_re.shape[1:], jnp.float32)
    advance = advance_back if backward else advance_fwd
    end_state, local_state = lax.scan(
        advance, (zeros_state, zeros_state), (vals_re, vals_im, keep_tile), reverse=backward
    )
    offsets = jnp.arange(block_len, dtype=jnp.float32)
    if backward:
        exponent = block_len - 1.0 - offsets
        through = jnp.flip(jnp.cumprod(jnp.flip(keep_tile, 0), axis=0), 0)
        kept_prod = jnp.concatenate([through[1:], jnp.ones_like(through[:1])], axis=0)
        whole_keep = through[0]
    else:
        exponent = offsets + 1.0
        kept_prod = jnp.cumprod(keep_tile, axis=0)
        whole_keep = kept_prod[-1]
    pow_re, pow_im = lam_power(decay_rate, mode_angle, exponent, conj_sign)
    full_re, full_im = lam_power(
        decay_rate, mode_angle, jnp.full((1,), float(block_len), jnp.float32), conj_sign
    )
    block_elems = (
        whole_keep[..., None] * full_re[0],
        whole_keep[..., None] * full_im[0],
        end_state[0],
        end_state[1],
    )
    inclusive = lax.associative_scan(compose, block_elems, reverse=backward, axis=0)
    summary = tuple((member[0] if backward else member[-1] for member in inclusive))
    return (local_state, (pow_re, pow_im, kept_prod), inclusive, summary)


def settle(local_state, weights, inclusive, carry_in, backward):
    pow_re, pow_im, kept_prod = weights
    apply_re, apply_im = complex_mul(
        inclusive[0], inclusive[1], carry_in[0][None], carry_in[1][None]
    )
    apply_re = apply_re + inclusive[2]
    apply_im = apply_im + inclusive[3]
    if backward:
        enter_re = jnp.concatenate([apply_re[1:], carry_in[0][None]], axis=0)
        enter_im = jnp.concatenate([apply_im[1:], carry_in[1][None]], axis=0)
    else:
        enter_re = jnp.concatenate([carry_in[0][None], apply_re[:-1]], axis=0)
        enter_im = jnp.concatenate([carry_in[1][None], apply_im[:-1]], axis=0)
    weight_re = pow_re[:, None, None, :] * kept_prod[..., None]
    weight_im = pow_im[:, None, None, :] * kept_prod[..., None]
    add_re, add_im = complex_mul(weight_re, weight_im, enter_re[None], enter_im[None])
    return (local_state[0] + add_re, local_state[1] + add_im)


def on_device(
    activations, cotangent, retain, dilation, conv_w, skip_gain, log_rate, mode_angle, w_in, w_out
):
    rec_count, time_steps, features = activations.shape
    mode_count = log_rate.shape[0]
    block_count = time_steps // block_span
    tail_rows = activations[:, time_steps - MAXLAG :, :]
    before_rows = from_behind(tail_rows, "tm", 1)
    extended = jnp.concatenate([before_rows, activations], axis=1)

    def tap_rows(k):
        start = MAXLAG - dilation[k]
        return lax.dynamic_slice_in_dim(extended, start, time_steps, 1).astype(jnp.float32)

    conv_out = jnp.zeros((rec_count, time_steps, features), jnp.float32)
    for k in range(TAPS):
        conv_out = conv_out + conv_w[k] * tap_rows(k)
    conv_b = conv_out.astype(jnp.bfloat16)
    conv_four = conv_b.reshape(rec_count, block_count, block_span, features)
    cot_four = cotangent.reshape(rec_count, block_count, block_span, features)
    decay_rate, radius, lam_re, lam_im, in_gain = decay_params(log_rate, mode_angle)
    keep_tile = jnp.transpose(retain.reshape(rec_count, block_count, block_span), (2, 1, 0))
    projected = jnp.einsum("rcjd,dm->jcrm", conv_four, w_in, preferred_element_type=jnp.float32)
    x_re = projected[..., :mode_count]
    x_im = projected[..., mode_count:]
    fwd_local, fwd_weights, fwd_incl, fwd_summary = local_sweep(
        in_gain * x_re, in_gain * x_im, keep_tile, decay_rate, mode_angle, lam_re, lam_im, False
    )
    back_proj = jnp.einsum("rcjd,md->jcrm", cot_four, w_out, preferred_element_type=jnp.float32)
    adj_local, adj_weights, adj_incl, adj_summary = local_sweep(
        back_proj[..., :mode_count],
        back_proj[..., mode_count:],
        keep_tile,
        decay_rate,
        mode_angle,
        lam_re,
        lam_im,
        True,
    )
    ones_state = jnp.ones((rec_count, mode_count), jnp.float32)
    zero_state = jnp.zeros((rec_count, mode_count), jnp.float32)
    identity = (ones_state, zero_state, zero_state, zero_state)
    state_scan = entering(
        (fwd_summary[0], fwd_summary[1], fwd_summary[2], fwd_summary[3]),
        "tm",
        compose,
        identity,
        False,
    )
    adjoint_scan = entering(
        (adj_summary[0], adj_summary[1], adj_summary[2], adj_summary[3]),
        "tm",
        compose,
        identity,
        True,
    )
    state_in = (state_scan[2], state_scan[3])
    adjoint_in = (adjoint_scan[2], adjoint_scan[3])
    h_re, h_im = settle(fwd_local, fwd_weights, fwd_incl, state_in, False)
    delta_re, delta_im = settle(adj_local, adj_weights, adj_incl, adjoint_in, True)
    h_b = jnp.concatenate([h_re, h_im], axis=-1).astype(jnp.bfloat16)
    raw_w_out = jnp.einsum("jcrm,rcjd->md", h_b, cot_four, preferred_element_type=jnp.float32)
    grad_x = jnp.concatenate([in_gain * delta_re, in_gain * delta_im], axis=-1).astype(jnp.bfloat16)
    raw_w_in = jnp.einsum("rcjd,jcrm->dm", conv_four, grad_x, preferred_element_type=jnp.float32)
    cot_float = cotangent.astype(jnp.float32)
    grad_conv = (
        jnp.einsum("jcrm,dm->rcjd", grad_x, w_in, preferred_element_type=jnp.float32).reshape(
            rec_count, time_steps, features
        )
        + skip_gain * cot_float
    )
    raw_skip = jnp.sum(cot_float * conv_out, axis=(0, 1))
    head_rows = grad_conv[:, :MAXLAG, :]
    after_rows = from_behind(head_rows.astype(jnp.bfloat16), "tm", -1).astype(head_rows.dtype)
    ext_grad = jnp.concatenate([grad_conv, after_rows], axis=1)
    grad_input = jnp.zeros((rec_count, time_steps, features), jnp.float32)
    tap_sums = []
    for k in range(TAPS):
        start = dilation[k]
        grad_input = grad_input + conv_w[k] * lax.dynamic_slice_in_dim(
            ext_grad, start, time_steps, 1
        )
        tap_sums.append(jnp.sum(grad_conv * tap_rows(k), axis=(0, 1)))
    raw_taps = jnp.stack(tap_sums)
    inner_keep = keep_tile[1:, ..., None]
    edge_re = jnp.concatenate([state_in[0][None], h_re[-1, :-1]], axis=0)
    edge_im = jnp.concatenate([state_in[1][None], h_im[-1, :-1]], axis=0)
    first_keep = keep_tile[0][..., None]
    lam_grad_re = jnp.sum(
        inner_keep * (delta_re[1:] * h_re[:-1] + delta_im[1:] * h_im[:-1]), axis=(0, 1, 2)
    )
    lam_grad_re = lam_grad_re + jnp.sum(
        first_keep * (delta_re[0] * edge_re + delta_im[0] * edge_im), axis=(0, 1)
    )
    lam_grad_im = jnp.sum(
        inner_keep * (delta_im[1:] * h_re[:-1] - delta_re[1:] * h_im[:-1]), axis=(0, 1, 2)
    )
    lam_grad_im = lam_grad_im + jnp.sum(
        first_keep * (delta_im[0] * edge_re - delta_re[0] * edge_im), axis=(0, 1)
    )
    gain_grad = jnp.sum(delta_re * x_re + delta_im * x_im, axis=(0, 1, 2))
    small_sums = lax.psum((raw_taps, raw_skip, lam_grad_re, lam_grad_im, gain_grad), ("tm", "rec"))
    merged = (
        lax.psum(raw_w_in.astype(jnp.bfloat16), "rec").astype(jnp.float32),
        lax.psum(raw_w_out.astype(jnp.bfloat16), "rec").astype(jnp.float32),
    )
    totals = (
        lax.psum_scatter(merged[0], "tm", scatter_dimension=0, tiled=True),
        lax.psum_scatter(merged[1], "tm", scatter_dimension=0, tiled=True),
    )
    total_rows = rec_count * time_steps * lax.axis_size("tm") * lax.axis_size("rec")
    scale = 1.0 / math.sqrt(total_rows)
    taps_total, skip_total, lam_total_re, lam_total_im, gain_total = small_sums
    radius_grad = (
        lam_total_re * jnp.cos(mode_angle)
        + lam_total_im * jnp.sin(mode_angle)
        - gain_total * radius / in_gain
    )
    grad_log_rate = -radius_grad * radius * decay_rate * scale
    grad_angle = (lam_total_im * lam_re - lam_total_re * lam_im) * scale
    return (
        grad_input.astype(jnp.bfloat16),
        taps_total * scale,
        skip_total * scale,
        grad_log_rate,
        grad_angle,
        totals[0] * scale,
        totals[1] * scale,
    )


def solution(mesh):
    placed = (
        P("rec", "tm", None),
        P("rec", "tm", None),
        P("rec", "tm"),
        P(),
        P(),
        P(),
        P(),
        P(),
        P(),
        P(),
    )
    return jax.shard_map(
        on_device,
        mesh=mesh,
        in_specs=placed,
        out_specs=(P("rec", "tm", None), P(), P(), P(), P(), P("tm", None), P("tm", None)),
        check_vma=False,
    )
```

profile of v0, /device:TPU:1, one launch (start us, length us, event | category | flops | bytes accessed | tf_op | source)
XLA Modules:
  0.0 1084.0 jit_solution(9771097109374445357)
XLA Ops:
  7.2 1.8 slice.779
  9.0 4.6 collective-permute-start.1
  16.7 2.1 convolution_bitcast_fusion.1
  18.8 1.5 fusion.106
  21.2 52.5 %while.72 = (s32[]{:T(128)}, f32[16,2,512]{2,1,0:T(2,128)S(1)}, f32[16,2,512]{2,1,0:T(2,128)S(1)}, f32[16,16,2,512]{3,1,2,0:T(8,128)S(1)}, f32[16,16,2,512]{3,1,...) while((s32[]{:T(128)}, f32[16,2,512]{2,1,0:T(2,128)S(1)}, ...), condition=%wide.region_1.2_spmd.clone, body=%wide.region_0.1_spmd.clone.sunk | while | flops 196612 | bytes 1188779 | solution.py:89
  29.6 1.1 constant_dynamic-slice_fusion.11
  36.1 1.1 constant_dynamic-slice_fusion.11
  42.7 1.1 constant_dynamic-slice_fusion.11
  81.9 1.9 pad.206
  83.8 1.4 slice_add_fusion.44
  85.2 1.3 pad_maximum_fusion.23
  86.4 1.9 pad.205
  88.3 1.9 pad.208
  90.2 1.3 pad_maximum_fusion.24
  91.5 1.9 pad.207
  93.4 1.3 add.727
  94.7 1.4 multiply_add_fusion.7
  96.1 1.3 add.729
  98.1 1.3 slice.871
  101.3 1.3 slice.899
  104.0 1.3 pad_maximum_fusion.26
  106.6 1.4 slice_add_fusion.28
  108.6 1.3 slice.918
  112.4 1.4 pad.210
  113.8 1.4 pad.212
  116.1 1.4 multiply_add_fusion.3
  118.3 1.4 pad.226
  119.8 1.4 pad.228
  126.7 1.7 fusion.114
  129.0 46.2 %all_gather.24 = f32[64,2,512]{2,1,0:T(2,128)S(1)} all-gather(f32[1,2,512]{2,1,0:T(2,128)S(1)} %slice_add_fusion.49), channel_id=1, replica_groups=mesh['tm'=64,'rec'=4] {'tm'}, dimensions={0}, use_global_device_ids=true | all-gather | bytes 266240 | tf_op jit(solution)/shard_map/all_gather | solution.py:25
  175.3 43.2 %all_gather.25 = f32[64,2,512]{2,1,0:T(2,128)S(1)} all-gather(f32[1,2,512]{2,1,0:T(2,128)S(1)} %slice_add_fusion.48), channel_id=1, replica_groups=mesh['tm'=64,'rec'=4] {'tm'}, dimensions={0}, use_global_device_ids=true | all-gather | bytes 266240 | tf_op jit(solution)/shard_map/all_gather | solution.py:25
  218.5 41.9 %all_gather.26 = f32[64,2,512]{2,1,0:T(2,128)S(1)} all-gather(f32[1,2,512]{2,1,0:T(2,128)S(1)} %slice_add_fusion.43), channel_id=1, replica_groups=mesh['tm'=64,'rec'=4] {'tm'}, dimensions={0}, use_global_device_ids=true | all-gather | bytes 266240 | tf_op jit(solution)/shard_map/all_gather | solution.py:25
  260.4 43.1 %all_gather.27 = f32[64,2,512]{2,1,0:T(2,128)S(1)} all-gather(f32[1,2,512]{2,1,0:T(2,128)S(1)} %slice_add_fusion.42), channel_id=1, replica_groups=mesh['tm'=64,'rec'=4] {'tm'}, dimensions={0}, use_global_device_ids=true | all-gather | bytes 266240 | tf_op jit(solution)/shard_map/all_gather | solution.py:25
  303.5 3.2 while.70
  320.6 1.6 fusion.78
  323.3 3.0 fusion.102
  328.0 3.0 slice_multiply_fusion
  331.0 1.1 broadcast.305.clone
  332.2 1.1 broadcast.305.clone2.2
  333.3 53.3 %while.73 = (s32[]{:T(128)}, f32[16,2,512]{2,1,0:T(2,128)S(1)}, f32[16,2,512]{2,1,0:T(2,128)S(1)}, f32[16,16,2,512]{3,1,2,0:T(8,128)}, f32[16,16,2,512]{3,1,2,0:...) while((s32[]{:T(128)}, f32[16,2,512]{2,1,0:T(2,128)S(1)}, ...), condition=%wide.region_18.19_spmd.clone, body=%wide.region_17.18_spmd.clone.sunk | while | flops 196611 | bytes 922391 | solution.py:89
  394.0 41.6 %all_gather.28 = f32[64,2,512]{2,1,0:T(2,128)S(1)} all-gather(f32[1,2,512]{2,1,0:T(2,128)S(1)} %slice_add_fusion.41), channel_id=1, replica_groups=mesh['tm'=64,'rec'=4] {'tm'}, dimensions={0}, use_global_device_ids=true | all-gather | bytes 266240 | tf_op jit(solution)/shard_map/all_gather | solution.py:25
  436.3 3.1 pad.343
  440.7 43.4 %all_gather.29 = f32[64,2,512]{2,1,0:T(2,128)S(1)} all-gather(f32[1,2,512]{2,1,0:T(2,128)S(1)} %slice_add_fusion.40), channel_id=1, replica_groups=mesh['tm'=64,'rec'=4] {'tm'}, dimensions={0}, use_global_device_ids=true | all-gather | bytes 266240 | tf_op jit(solution)/shard_map/all_gather | solution.py:25
  484.8 3.0 pad.339
  487.8 3.1 pad.261
  490.9 2.8 pad.262
  494.4 45.0 %all_gather.30 = f32[64,2,512]{2,1,0:T(2,128)} all-gather(f32[1,2,512]{2,1,0:T(2,128)S(1)} %slice_add_fusion.35), channel_id=1, replica_groups=mesh['tm'=64,'rec'=4] {'tm'}, dimensions={0}, use_global_device_ids=true | all-gather | bytes 266240 | tf_op jit(solution)/shard_map/all_gather | solution.py:25
  540.2 3.1 pad.345
  543.2 3.1 pad.263
  546.3 2.8 pad.669
  549.8 47.0 %all_gather.31 = f32[64,2,512]{2,1,0:T(2,128)} all-gather(f32[1,2,512]{2,1,0:T(2,128)S(1)} %slice_add_fusion.34), channel_id=1, replica_groups=mesh['tm'=64,'rec'=4] {'tm'}, dimensions={0}, use_global_device_ids=true | all-gather | bytes 266240 | tf_op jit(solution)/shard_map/all_gather | solution.py:25
  597.6 1.2 fusion.107
  601.1 2.0 bitcast_convert_fusion.1
  603.1 1.8 fusion.96
  604.9 1.9 bitcast_convert_fusion
  625.3 86.0 %all-reduce.71.cloned.1.call-done = (bf16[512,1024]{1,0:T(8,128)(2,1)}, bf16[1024,512]{1,0:T(8,128)(2,1)}) async-done(((bf16[512,1024]{1,0:T(8,128)(2,1)}, bf16[1024,512]{1,0:T(8,128)(2,1)}), (bf16[512,1024]{1,0:T(8,128)(2,1)}, bf16[1024,512]{1,0:T(8,128)(2,1)})) %all-reduce.71.cloned.1.call-update) | async-done | bytes 2097168 | tf_op jit(solution)/shard_map/psum | solution.py:239
  711.3 2.8 convert_element_type.79
  714.2 1.9 convolution_bitcast_fusion.2
  716.8 2.1 fusion.28
  718.9 2.6 collective-permute-start
  722.3 76.8 %all-reduce.66 = (f32[9,512]{1,0:T(8,128)S(1)}, f32[512]{0:T(512)S(1)}, f32[512]{0:T(512)S(1)}, f32[512]{0:T(512)S(1)}, f32[512]{0:T(512)S(1)}) all-reduce(f32[9,512]{1,0:T(8,128)S(1)} %stack.39, f32[512]{0:T(512)S(1)} %get-tuple-element.746, f32[512]{0:T(512)S(1)} %copy-done.68, ...), channel_id=1, replica_groups=mesh['tm'=64,'rec'=4] {'tm','rec'}, use_global_device_ids=true, to_apply=%region_14.15 | all-reduce | flops 6656 | bytes 53248 | tf_op jit(solution)/shard_map/psum | solution.py:237
  801.1 8.6 fusion.40
  809.7 265.2 %all-reduce.72 = f32[512,1024]{1,0:T(8,128)S(1)} all-reduce(bf16[512,1024]{1,0:T(8,128)(2,1)} %get-tuple-element.712), channel_id=2, replica_groups=mesh['tm'=64,'rec'=4] {'tm'}, use_global_device_ids=true, to_apply=%region_31.32.clone | all-reduce | flops 524288 | bytes 3145728
  1075.5 1.4 broadcast_multiply_fusion.4
  (625 shorter events, 157.1 us)
Async XLA Ops:
  7.2 319.2 %copy-start = (bf16[512,1024]{1,0:T(8,128)(2,1)S(1)}, bf16[512,1024]{1,0:T(8,128)(2,1)}, u32[]{:S(2)}) copy-start(bf16[512,1024]{1,0:T(8,128)(2,1)} %param.26) | copy-start | bytes 3145732
  7.2 704.1 %all-reduce.71.cloned.1.call-start = ((), (), s32[]{:S(2)}) async-start(), calls=%async_computation.2 | async-start | bytes 4194304 | tf_op jit(solution)/shard_map/psum | solution.py:239
  9.0 313.3 %collective-permute-start.1 = (bf16[2,128,512]{2,1,0:T(8,128)(2,1)}, bf16[2,128,512]{2,1,0:T(8,128)(2,1)}, u32[]{:S(2)}, u32[]{:S(2)}) collective-permute-start(bf16[2,128,512]{2,1,0:T(8,128)(2,1)} %slice.779), channel_id=1, source_target_pairs={{0,4},{4,8},{8,12},{12,16},{16,20},{20,24},{24,28},{28,32},{32,36}... | collective-permute-start | bytes 786440 | tf_op jit(solution)/shard_map/ppermute | solution.py:18
  16.6 3.7 copy-start.41
  16.6 3.7 copy-start.43
  73.7 43.8 %copy-start.8 = (f32[16,16,2,512]{3,1,2,0:T(8,128)}, f32[16,16,2,512]{3,1,2,0:T(8,128)S(1)}, u32[]{:S(2)}) copy-start(f32[16,16,2,512]{3,1,2,0:T(8,128)S(1)} %get-tuple-element.464) | copy-start | bytes 3145732
  73.7 43.8 %copy-start.10 = (f32[16,16,2,512]{3,1,2,0:T(8,128)}, f32[16,16,2,512]{3,1,2,0:T(8,128)S(1)}, u32[]{:S(2)}) copy-start(f32[16,16,2,512]{3,1,2,0:T(8,128)S(1)} %get-tuple-element.469) | copy-start | bytes 3145732
  74.8 1.8 copy-start.17
  77.3 3.9 copy-start.22
  77.4 3.2 copy-start.23
  77.4 3.7 copy-start.30
  77.5 3.7 copy-start.31
  77.5 3.7 copy-start.34
  77.5 3.7 copy-start.35
  77.5 3.7 copy-start.36
  77.5 3.7 copy-start.37
  117.5 8.5 copy-start.64
  117.5 10.9 %copy-start.65 = (f32[9,512]{1,0:T(8,128)S(1)}, f32[9,512]{1,0:T(8,128)}, u32[]{:S(2)}) copy-start(f32[9,512]{1,0:T(8,128)} %param.22) | copy-start | bytes 55300
  124.8 193.6 %copy-start.18 = (f32[16,16,2]{2,1,0:T(8,128)S(1)}, f32[16,16,2]{2,1,0:T(8,128)}, u32[]{:S(2)}) copy-start(f32[16,16,2]{2,1,0:T(8,128)} %copy-done.17) | copy-start | bytes 6148
  125.8 193.4 %slice-start = ((f32[16,16,2]{2,1,0:T(8,128)}), f32[15,16,2]{2,1,0:T(8,128)S(1)}, s32[]{:S(2)}) async-start(f32[16,16,2]{2,1,0:T(8,128)} %copy-done.21), calls=%async_computation.3 | async-start | bytes 245760 | tf_op jit(solution)/shard_map/slice | solution.py:96
  126.2 194.4 %copy-start.40 = (f32[512]{0:T(512)S(1)}, f32[512]{0:T(512)}, u32[]{:S(2)}) copy-start(f32[512]{0:T(512)} %param.25) | copy-start | bytes 6148
  129.0 194.2 %copy-start.45 = (f32[1,512]{1,0:T(1,128)}, f32[1,512]{1,0:T(1,128)S(1)}, u32[]{:S(2)}) copy-start(f32[1,512]{1,0:T(1,128)S(1)} %get-tuple-element.816) | copy-start | bytes 6148
  129.0 194.2 %copy-start.47 = (f32[1,512]{1,0:T(1,128)}, f32[1,512]{1,0:T(1,128)S(1)}, u32[]{:S(2)}) copy-start(f32[1,512]{1,0:T(1,128)S(1)} %get-tuple-element.817) | copy-start | bytes 6148
  175.3 147.9 %copy-start.16 = (bf16[2,256,512]{2,1,0:T(8,128)(2,1)S(1)}, bf16[2,256,512]{2,1,0:T(8,128)(2,1)}, u32[]{:S(2)}) copy-start(bf16[2,256,512]{2,1,0:T(8,128)(2,1)} %param.18) | copy-start | bytes 1572868
  306.7 13.9 %copy-start.70 = (f32[16]{0:T(128)S(1)}, f32[16]{0:T(128)}, u32[]{:S(2)}) copy-start(f32[16]{0:T(128)} %get-tuple-element.878) | copy-start | bytes 196
  306.7 13.9 %copy-start.71 = (f32[16]{0:T(128)S(1)}, f32[16]{0:T(128)}, u32[]{:S(2)}) copy-start(f32[16]{0:T(128)} %get-tuple-element.879) | copy-start | bytes 196
  306.8 16.5 %copy-start.49 = (f32[1,512]{1,0:T(1,128)S(1)}, f32[1,512]{1,0:T(1,128)}, u32[]{:S(2)}) copy-start(f32[1,512]{1,0:T(1,128)} %get-tuple-element.818) | copy-start | bytes 6148
  306.8 16.5 %copy-start.51 = (f32[1,512]{1,0:T(1,128)S(1)}, f32[1,512]{1,0:T(1,128)}, u32[]{:S(2)}) copy-start(f32[1,512]{1,0:T(1,128)} %get-tuple-element.819) | copy-start | bytes 6148
  306.8 16.5 %copy-start.53 = (f32[1,512]{1,0:T(1,128)S(1)}, f32[1,512]{1,0:T(1,128)}, u32[]{:S(2)}) copy-start(f32[1,512]{1,0:T(1,128)} %get-tuple-element.820) | copy-start | bytes 6148
  306.8 16.5 %copy-start.55 = (f32[1,512]{1,0:T(1,128)S(1)}, f32[1,512]{1,0:T(1,128)}, u32[]{:S(2)}) copy-start(f32[1,512]{1,0:T(1,128)} %get-tuple-element.821) | copy-start | bytes 6148
  306.8 16.5 %copy-start.57 = (f32[1,512]{1,0:T(1,128)S(1)}, f32[1,512]{1,0:T(1,128)}, u32[]{:S(2)}) copy-start(f32[1,512]{1,0:T(1,128)} %get-tuple-element.822) | copy-start | bytes 6148
  306.8 16.5 %copy-start.59 = (f32[1,512]{1,0:T(1,128)S(1)}, f32[1,512]{1,0:T(1,128)}, u32[]{:S(2)}) copy-start(f32[1,512]{1,0:T(1,128)} %get-tuple-element.823) | copy-start | bytes 6148
  306.8 16.5 %copy-start.61 = (f32[1,512]{1,0:T(1,128)S(1)}, f32[1,512]{1,0:T(1,128)}, u32[]{:S(2)}) copy-start(f32[1,512]{1,0:T(1,128)} %get-tuple-element.824) | copy-start | bytes 6148
  331.0 2.3 copy-start.38
  493.7 45.7 %copy-start.29 = (f32[16,2,512]{2,1,0:T(2,128)}, f32[16,2,512]{2,1,0:T(2,128)S(1)}, u32[]{:S(2)}) copy-start(f32[16,2,512]{2,1,0:T(2,128)S(1)} %pad.262) | copy-start | bytes 196612
  597.6 2.3 copy-start.1
  600.9 2.2 copy-start.15
  601.0 2.0 copy-start.4
  601.1 2.0 copy-start.5
  601.1 2.0 copy-start.32
  601.1 2.0 copy-start.33
  603.1 1.9 copy-start.19
  606.8 17.2 %copy-start.72 = (u32[256]{0:T(256)S(1)}, u32[256]{0:T(256)}, u32[]{:S(2)}) copy-start(u32[256]{0:T(256)} %constant.291) | copy-start | bytes 3076
  606.8 468.7 %reduce-scatter.2.cloned.1.call-start = ((), (), s32[]{:S(2)}) async-start(), calls=%async_computation.1 | async-start | bytes 2129920 | tf_op jit(solution)/shard_map/reduce_scatter | solution.py:244
  714.1 2.6 copy-start.12
  714.1 2.6 copy-start.20
  714.2 2.6 copy-start.69
  716.7 4.8 copy-start.7
  716.7 4.8 copy-start.6
  716.7 4.8 copy-start.2
  718.9 3.3 copy-start.3
  718.9 82.0 %collective-permute-start = (bf16[2,128,512]{2,1,0:T(8,128)(2,1)S(1)}, bf16[2,128,512]{2,1,0:T(8,128)(2,1)S(1)}, u32[]{:S(2)}, u32[]{:S(2)}) collective-permute-start(bf16[2,128,512]{2,1,0:T(8,128)(2,1)S(1)} %slice.1537), channel_id=1, source_target_pairs={{4,0},{8,4},{12,8},{16,12},{20,16},{24,20},{28,24},{32,28},{36,32}... | collective-permute-start | bytes 786440 | tf_op jit(solution)/shard_map/ppermute | solution.py:18
  721.7 77.5 %copy-start.42 = (f32[512]{0:T(512)S(1)}, f32[512]{0:T(512)}, u32[]{:S(2)}) copy-start(f32[512]{0:T(512)} %copy-done.41) | copy-start | bytes 6148
  721.7 77.5 %copy-start.44 = (f32[512]{0:T(512)S(1)}, f32[512]{0:T(512)}, u32[]{:S(2)}) copy-start(f32[512]{0:T(512)} %copy-done.43) | copy-start | bytes 6148
  721.7 77.4 %copy-start.67 = (f32[512]{0:T(512)S(1)}, f32[512]{0:T(512)}, u32[]{:S(2)}) copy-start(f32[512]{0:T(512)} %param.24) | copy-start | bytes 6148
  721.7 79.3 %copy-start.46 = (f32[1,512]{1,0:T(1,128)S(1)}, f32[1,512]{1,0:T(1,128)}, u32[]{:S(2)}) copy-start(f32[1,512]{1,0:T(1,128)} %copy-done.45) | copy-start | bytes 6148
  721.7 79.3 %copy-start.48 = (f32[1,512]{1,0:T(1,128)S(1)}, f32[1,512]{1,0:T(1,128)}, u32[]{:S(2)}) copy-start(f32[1,512]{1,0:T(1,128)} %copy-done.47) | copy-start | bytes 6148
  721.7 79.3 %copy-start.50 = (f32[1,512]{1,0:T(1,128)S(1)}, f32[1,512]{1,0:T(1,128)}, u32[]{:S(2)}) copy-start(f32[1,512]{1,0:T(1,128)} %get-tuple-element.818) | copy-start | bytes 6148
  721.7 79.3 %copy-start.52 = (f32[1,512]{1,0:T(1,128)S(1)}, f32[1,512]{1,0:T(1,128)}, u32[]{:S(2)}) copy-start(f32[1,512]{1,0:T(1,128)} %get-tuple-element.819) | copy-start | bytes 6148
  721.7 79.3 %copy-start.54 = (f32[1,512]{1,0:T(1,128)S(1)}, f32[1,512]{1,0:T(1,128)}, u32[]{:S(2)}) copy-start(f32[1,512]{1,0:T(1,128)} %get-tuple-element.820) | copy-start | bytes 6148
  721.7 79.3 %copy-start.56 = (f32[1,512]{1,0:T(1,128)S(1)}, f32[1,512]{1,0:T(1,128)}, u32[]{:S(2)}) copy-start(f32[1,512]{1,0:T(1,128)} %get-tuple-element.821) | copy-start | bytes 6148
  721.8 79.3 %copy-start.58 = (f32[1,512]{1,0:T(1,128)S(1)}, f32[1,512]{1,0:T(1,128)}, u32[]{:S(2)}) copy-start(f32[1,512]{1,0:T(1,128)} %get-tuple-element.822) | copy-start | bytes 6148
  721.8 79.3 %copy-start.60 = (f32[1,512]{1,0:T(1,128)S(1)}, f32[1,512]{1,0:T(1,128)}, u32[]{:S(2)}) copy-start(f32[1,512]{1,0:T(1,128)} %get-tuple-element.823) | copy-start | bytes 6148
  721.8 79.3 %copy-start.62 = (f32[1,512]{1,0:T(1,128)S(1)}, f32[1,512]{1,0:T(1,128)}, u32[]{:S(2)}) copy-start(f32[1,512]{1,0:T(1,128)} %get-tuple-element.824) | copy-start | bytes 6148
  (14 other events, 15.8 us)
Sparse Core Ops, SparseCore 0:
  606.9 104.2 all-reduce.70
  715.9 135.9 reduce-scatter.1
where the time goes:
time: 1100 us; the launch traced here: 1080 us
  blocking collectives  693 us (63%)
  local copies, waits for them, and re-layouts  165 us (15%)
  waiting for transfers between devices  86 us (8%)
  other arithmetic  76.2 us (7%)
  between operations  44.7 us (4%)
    all_gather x8, blocking collectives, entering(): gathered = jax.tree.map(lambda a: lax.all_gather(a, axis), part)  351 us
    unnamed x1, blocking collectives  265 us
    psum x1, waiting for transfers between devices, on_device(): lax.psum(raw_w_in.astype(jnp.bfloat16), 'rec').astype(jnp.float32)  86 us
    psum x1, blocking collectives, on_device(): lax.psum((raw_taps, raw_skip, lam_grad_re, lam_grad_im, gain_grad), ('tm'...  76.8 us
    dynamic_slice x64, local copies, waits for them, and re-layouts, local_sweep(): lax.scan(advance, (zeros_state, zeros_state), (vals_re, vals_im, keep_til...  62.1 us
    pad x45, local copies, waits for them, and re-layouts, local_sweep(): lax.associative_scan(compose, block_elems, reverse=backward, axis=0)  25.1 us
  transfers between devices with their start and end apart: 4, of which 1 were waited for; matrix products, arithmetic and copies ran while one was open for 13% of the time, Pallas kernels for 0%

commit v1 on v0

v1 whole, which is shorter than its diff:
```python
import functools
import math

import jax
import jax.numpy as jnp
from jax import lax
from jax.experimental import pallas as pl
from jax.experimental.pallas import tpu as pltpu
from jax.sharding import PartitionSpec as P

TAPS = 9
MAXLAG = 128
NB = 8
PIECE = 16
F32 = jnp.float32
BF16 = jnp.bfloat16


class Sizes:
    def __init__(self, tm, rec, time_steps, features, lag):
        self.core = 2
        self.nx = rec
        self.ny = 4 if tm >= 64 else 2
        self.nz = tm // (self.core * self.ny)
        self.group = self.core * self.ny
        self.recs = 2
        self.t = time_steps
        self.d = features
        self.lag = lag
        self.bl = time_steps // NB
        self.lw = features // 4
        self.half = features // 2
        self.xw = features // rec
        self.sw = features // self.ny
        self.chunk = min(64, time_steps)


def mul(ar, ai, br, bi):
    return ar * br - ai * bi, ar * bi + ai * br


def square_times(re, im, times):
    for _ in range(times):
        re, im = re * re - im * im, 2.0 * (re * im)
    return re, im


def log2(n):
    return n.bit_length() - 1


def kernel(
    s,
    dil_ref,
    retain_ref,
    convw_ref,
    par_ref,
    act_hbm,
    cot_hbm,
    win_hbm,
    wout_hbm,
    gin_ref,
    taps_ref,
    skip_ref,
    rate_ref,
    angle_ref,
    gwin_ref,
    gwout_ref,
    act_v,
    cot_v,
    win_v,
    wout_v,
    halo_v,
    ext_act,
    ext_grad,
    cotp_v,
    convb_v,
    convp_v,
    keep_v,
    e_v,
    x_v,
    hb_v,
    gx_v,
    head_v,
    ghalo_v,
    w1_v,
    w2_v,
    scan_a,
    scan_b,
    small_v,
    ssend,
    srecv_core,
    ssum_core,
    srecv_y,
    sx_v,
    sz_v,
    sall_v,
    send_w,
    recv_w,
    chip_w,
    recv1_w0,
    recv1_w1,
    sum1_w0,
    sum1_w1,
    recv2_w,
    sum2_w,
    recv3_w,
    full_w,
    in_sem,
    halo_sem,
    a_send,
    a_recv,
    b_send,
    b_recv,
    wc_sem,
    w1_send,
    w1_recv,
    w2_send,
    w2_recv,
    w3_send,
    w3_recv,
    w4_send,
    w4_recv,
    sc_sem,
    sy_send,
    sy_recv,
    sx_send,
    sx_recv,
    sz_send,
    sz_recv,
    sg_send,
    sg_recv,
    sf_sem,
):
    t_len, d, half, lw = s.t, s.d, s.half, s.lw
    tm = lax.axis_index("tm")
    rec = lax.axis_index("rec")
    core = lax.rem(tm, s.core)
    y = lax.rem(tm // s.core, s.ny)
    z = tm // s.group
    spot = lax.rem(tm, s.group)
    tm_count = s.nz * s.group
    other = 1 - core

    def at(tm_to, rec_to):
        return (tm_to, rec_to)

    def at_group(o):
        return at(z * s.group + lax.rem(spot + o, s.group), rec)

    def at_core():
        return at(tm + 1 - 2 * core, rec)

    def at_y(o):
        return at(z * s.group + lax.rem(y + o, s.ny) * s.core + core, rec)

    def at_z(o):
        return at(lax.rem(z + o, s.nz) * s.group + spot, rec)

    def at_x(o):
        return at(tm, lax.rem(rec + o, s.nx))

    def at_tm(o):
        return at(lax.rem(tm + o + tm_count, tm_count), rec)

    def remote(src, dst, ssem, rsem, to):
        return pltpu.make_async_remote_copy(
            src_ref=src,
            dst_ref=dst,
            send_sem=ssem,
            recv_sem=rsem,
            device_id=to,
            device_id_type=pl.DeviceIdType.MESH,
        )

    loads = [
        pltpu.make_async_copy(src, dst, in_sem.at[i])
        for i, (src, dst) in enumerate(
            ((cot_hbm, cot_v), (wout_hbm, wout_v), (act_hbm, act_v), (win_hbm, win_v))
        )
    ]
    for load in loads:
        load.start()
    scan_b[...] = jnp.zeros_like(scan_b)
    barrier = pltpu.get_barrier_semaphore()
    partners = (
        [at_group(o) for o in range(1, s.group)]
        + [at_z(o) for o in range(1, s.nz)]
        + [at_x(o) for o in range(1, s.nx)]
        + [at_tm(1), at_tm(-1)]
    )
    for partner in partners:
        pl.semaphore_signal(
            barrier, inc=1, device_id=partner, device_id_type=pl.DeviceIdType.MESH
        )

    row = lax.broadcasted_iota(jnp.int32, (t_len, t_len), 0)
    col = lax.broadcasted_iota(jnp.int32, (t_len, t_len), 1)
    chosen = col == lax.rem(row, NB) * s.bl + row // NB
    order = jnp.where(chosen, 1.0, 0.0).astype(BF16)
    for r in range(s.recs):
        picked = jnp.sum(
            jnp.where(chosen, retain_ref[r : r + 1, :], 0.0), axis=1, keepdims=True
        )
        keep_v[r] = jnp.broadcast_to(picked, (t_len, lw))

    lam_re = par_ref[0:1, :]
    lam_im = par_ref[1:2, :]
    in_gain = par_ref[2:3, :]
    block_pow = [square_times(lam_re, lam_im, log2(s.bl))]
    for _ in range(2):
        block_pow.append(square_times(*block_pow[-1], 1))
    dev_pow = square_times(*block_pow[-1], 1)
    plane_pow = square_times(*dev_pow, log2(s.group))

    def packed(v):
        pair = jnp.concatenate([v[:, :half], v[:, half:]], axis=0)
        return jnp.concatenate([pair] * s.recs, axis=0)

    dev_pack = (packed(dev_pow[0]), packed(dev_pow[1]))
    plane_pack = (packed(plane_pow[0]), packed(plane_pow[1]))
    sub_row = lax.broadcasted_iota(jnp.int32, (NB, d), 0)
    sub_row_k = lax.broadcasted_iota(jnp.int32, (NB, lw), 0)

    def power_table(index):
        re = jnp.ones((NB, d), F32)
        im = jnp.zeros((NB, d), F32)
        for bit, (pr, pi) in zip((1, 2, 4), block_pow):
            nr, ni = mul(re, im, pr, pi)
            here = lax.rem(index // bit, 2) == 1
            re = jnp.where(here, nr, re)
            im = jnp.where(here, ni, im)
        return re, im

    def wide(k):
        return jnp.concatenate([k] * (d // k.shape[1]), axis=1)

    def block_scan(e_re, e_im, k, sign):
        for span, (pr, pi) in zip((1, 2, 4), block_pow):
            shift = span if sign > 0 else NB - span
            pi = sign * pi
            n_re = pltpu.roll(e_re, shift, 0)
            n_im = pltpu.roll(e_im, shift, 0)
            n_k = pltpu.roll(k, shift, 0)
            there = sub_row >= span if sign > 0 else sub_row < NB - span
            there_k = sub_row_k >= span if sign > 0 else sub_row_k < NB - span
            m_re, m_im = mul(pr, pi, n_re, n_im)
            k_wide = wide(k)
            e_re = e_re + jnp.where(there, k_wide * m_re, 0.0)
            e_im = e_im + jnp.where(there, k_wide * m_im, 0.0)
            k = jnp.where(there_k, k * n_k, k)
        return e_re, e_im, k

    def summarize(way, scans):
        last = NB - 1 if way == 0 else 0
        for r in range(s.recs):
            e_re, e_im, k = scans[r]
            for part, v in enumerate((e_re, e_im)):
                for h in range(2):
                    at_row = part * 4 + r * 2 + h
                    scan_a[way, spot, at_row : at_row + 1, 0:half] = v[
                        last : last + 1, h * half : (h + 1) * half
                    ]
                    scan_a[way, spot, at_row : at_row + 1, half : half + lw] = k[
                        last : last + 1, :
                    ]

    def copy_a(way, o, back=False):
        held = scan_a.at[way, lax.rem(spot + s.group - o, s.group) if back else spot]
        return remote(held, held, a_send.at[way, o], a_recv.at[way, o], at_group(o))

    def copy_b(way, o, back=False):
        held = scan_b.at[way, lax.rem(z + s.nz - o, s.nz) if back else z]
        return remote(held, held, b_send.at[way, o], b_recv.at[way, o], at_z(o))

    def sends_b(way, o):
        return z + o < s.nz if way == 0 else z + o >= s.nz

    def gets_b(way, o):
        return z - o >= 0 if way == 0 else z - o < 0

    def start_a(way):
        for o in range(1, s.group):
            copy_a(way, o).start()

    def advance(slot, state, pack, way):
        sign = 1.0 if way == 0 else -1.0
        k = slot[0:4, half : half + lw]
        k = jnp.concatenate([k] * (half // lw), axis=1)
        m_re, m_im = mul(pack[0], sign * pack[1], state[0], state[1])
        return slot[0:4, 0:half] + k * m_re, slot[4:8, 0:half] + k * m_im

    def in_order(count, way):
        return range(count) if way == 0 else range(count - 1, -1, -1)

    def plane_step(way):
        for o in range(1, s.group):
            copy_a(way, o, True).wait_recv()
        state = (jnp.zeros((4, half), F32), jnp.zeros((4, half), F32))
        k_all = jnp.ones((4, lw), F32)
        for i in in_order(s.group, way):
            slot = scan_a[way, i]
            state = advance(slot, state, dev_pack, way)
            k_all = k_all * slot[0:4, half : half + lw]
        scan_b[way, z, 0:4, 0:half] = state[0]
        scan_b[way, z, 4:8, 0:half] = state[1]
        scan_b[way, z, 0:4, half : half + lw] = k_all
        scan_b[way, z, 4:8, half : half + lw] = k_all
        for o in range(1, s.nz):

            @pl.when(sends_b(way, o))
            def _():
                copy_b(way, o).start()

    def entering(way):
        for o in range(1, s.nz):

            @pl.when(gets_b(way, o))
            def _():
                copy_b(way, o, True).wait_recv()

        state = (jnp.zeros((4, half), F32), jnp.zeros((4, half), F32))
        for i in in_order(s.nz, way):
            moved = advance(scan_b[way, i], state, plane_pack, way)
            use = i < z if way == 0 else i > z
            state = tuple(jnp.where(use, m, o) for m, o in zip(moved, state))
        for i in in_order(s.group, way):
            moved = advance(scan_a[way, i], state, dev_pack, way)
            use = i < spot if way == 0 else i > spot
            state = tuple(jnp.where(use, m, o) for m, o in zip(moved, state))
        return state

    def block_entry(way, scans, state):
        sign = 1.0 if way == 0 else -1.0
        index = sub_row if way == 0 else NB - 1 - sub_row
        pw_re, pw_im = power_table(index)
        pw_im = sign * pw_im
        shift = 1 if way == 0 else NB - 1
        out = []
        for r in range(s.recs):
            s_re, s_im = (
                jnp.concatenate([v[2 * r : 2 * r + 1], v[2 * r + 1 : 2 * r + 2]], axis=1)
                for v in state
            )
            e_re, e_im, k = scans[r]
            m_re, m_im = mul(pw_re, pw_im, s_re, s_im)
            k_wide = wide(pltpu.roll(k, shift, 0))
            first = index == 0
            out.append(
                (
                    jnp.where(first, s_re, pltpu.roll(e_re, shift, 0) + k_wide * m_re),
                    jnp.where(first, s_im, pltpu.roll(e_im, shift, 0) + k_wide * m_im),
                )
            )
        return out

    lr = jnp.broadcast_to(lam_re, (NB, d))
    li = jnp.broadcast_to(lam_im, (NB, d))
    gain = jnp.broadcast_to(in_gain, (NB, d))
    zero = jnp.zeros((NB, d), F32)

    def rows(j):
        return pl.ds(pl.multiple_of(j * NB, NB), NB)

    def rows2(i):
        return pl.ds(pl.multiple_of(i * 2 * NB, 2 * NB), 2 * NB)

    loads[0].wait()
    loads[1].wait()
    nt = (((1,), (1,)), ((), ()))
    tn = (((0,), (0,)), ((), ()))
    for r in range(s.recs):
        cotp_v[r] = jnp.dot(order, cot_v[r], preferred_element_type=F32).astype(BF16)
        e_v[r] = lax.dot_general(cotp_v[r], wout_v[...], nt, preferred_element_type=F32)

    pl.semaphore_wait(barrier, len(partners))
    act_halo = remote(
        act_hbm.at[:, pl.ds(t_len - s.lag, s.lag), :],
        halo_v,
        halo_sem.at[0],
        halo_sem.at[1],
        at_tm(1),
    )
    act_halo.start()

    def adj_first(i, carry):
        j = s.bl - 1 - i
        new = []
        for r in range(s.recs):
            p_re, p_im, k_all = carry[r]
            k = keep_v[r, rows(j), :]
            k4 = wide(k)
            d_re = e_v[r, rows(j), 0:d] + p_re
            d_im = e_v[r, rows(j), d : 2 * d] + p_im
            m_re, m_im = mul(lr, -li, d_re, d_im)
            new.append((k4 * m_re, k4 * m_im, k_all * k))
        return tuple(new)

    ones_k = jnp.ones((NB, lw), F32)
    ends = lax.fori_loop(0, s.bl, adj_first, ((zero, zero, ones_k),) * s.recs)
    keeps = [ends[r][2] for r in range(s.recs)]
    adj_scans = [block_scan(*ends[r], -1.0) for r in range(s.recs)]
    summarize(1, adj_scans)
    start_a(1)

    loads[2].wait()
    for r in range(s.recs):
        for l in range(4):
            ext_act[r, l, s.lag : s.lag + t_len, :] = act_v[
                r, :, l * lw : (l + 1) * lw
            ].astype(F32)
    act_halo.wait_recv()
    for r in range(s.recs):
        for l in range(4):
            before = halo_v[r, :, l * lw : (l + 1) * lw].astype(F32)
            ext_act[r, l, 0 : s.lag, :] = jnp.where(tm > 0, before, 0.0)

    per_rec = t_len // s.chunk

    def fold(v):
        return jnp.sum(v.reshape(s.chunk // 8, 8, lw), axis=0)

    for l in range(4):
        lanes = slice(l * lw, (l + 1) * lw)
        taps_l = [convw_ref[k : k + 1, lanes] for k in range(TAPS)]

        def conv_step(i, acc):
            r = i // per_rec
            base = pl.multiple_of(lax.rem(i, per_rec) * s.chunk, s.chunk)
            out = jnp.zeros((s.chunk, lw), F32)
            for k in range(TAPS):
                out += taps_l[k] * ext_act[r, l, pl.ds(base + s.lag - dil_ref[k], s.chunk), :]
            convb_v[r, pl.ds(base, s.chunk), lanes] = out.astype(BF16)
            return acc + fold(out * cot_v[r, pl.ds(base, s.chunk), lanes].astype(F32))

        skip_acc = lax.fori_loop(0, s.recs * per_rec, conv_step, jnp.zeros((8, lw), F32))
        small_v[9:10, lanes] = jnp.sum(skip_acc, axis=0, keepdims=True)

    plane_step(1)

    loads[3].wait()
    for r in range(s.recs):
        convp_v[r] = jnp.dot(order, convb_v[r], preferred_element_type=F32).astype(BF16)
        x_v[r] = jnp.dot(convp_v[r], win_v[...], preferred_element_type=F32)

    def fwd_first(j, carry):
        new = []
        for r in range(s.recs):
            h_re, h_im = carry[r]
            k4 = wide(keep_v[r, rows(j), :])
            m_re, m_im = mul(lr, li, h_re, h_im)
            new.append(
                (
                    k4 * m_re + gain * x_v[r, rows(j), 0:d],
                    k4 * m_im + gain * x_v[r, rows(j), d : 2 * d],
                )
            )
        return tuple(new)

    ends = lax.fori_loop(0, s.bl, fwd_first, ((zero, zero),) * s.recs)
    fwd_scans = [block_scan(*ends[r], keeps[r], 1.0) for r in range(s.recs)]
    summarize(0, fwd_scans)
    start_a(0)

    entry = block_entry(1, adj_scans, entering(1))

    def adj_second(i, carry):
        i = s.bl // 2 - 1 - i
        new = []
        for r in range(s.recs):
            p_re, p_im = carry[r]
            held = [None, None]
            for sub in (1, 0):
                j = 2 * i + sub
                k4 = wide(keep_v[r, rows(j), :])
                d_re = e_v[r, rows(j), 0:d] + p_re
                d_im = e_v[r, rows(j), d : 2 * d] + p_im
                e_v[r, rows(j), 0:d] = d_re
                e_v[r, rows(j), d : 2 * d] = d_im
                held[sub] = (gain * d_re, gain * d_im)
                m_re, m_im = mul(lr, -li, d_re, d_im)
                p_re, p_im = k4 * m_re, k4 * m_im
            for part in range(2):
                gx_v[r, rows2(i), part * d : (part + 1) * d] = jnp.concatenate(
                    [held[0][part], held[1][part]], axis=0
                ).astype(BF16)
            new.append((p_re, p_im))
        return tuple(new)

    lax.fori_loop(0, s.bl // 2, adj_second, tuple(entry))

    plane_step(0)

    pieces = s.nz * s.ny

    def piece_in(g, c):
        at_row = pl.ds(pl.multiple_of((g * 2 + c) * 8, 8), 8)
        return jnp.concatenate([w1_v[at_row, 0:d], w1_v[at_row, d : 2 * d]], axis=0)

    def piece_out(g, c):
        return w2_v[pl.ds(pl.multiple_of((g * 2 + c) * PIECE, PIECE), PIECE), :]

    piece = (piece_in, piece_out)

    def core_copy(w):
        return remote(send_w.at[w], recv_w.at[w], wc_sem.at[w, 0], wc_sem.at[w, 1], at_core())

    def send_core(w):
        def one(g, _):
            send_w[w, g] = piece[w](g, other).astype(BF16)
            return 0

        lax.fori_loop(0, pieces, one, 0)
        core_copy(w).start()

    recv1 = (recv1_w0, recv1_w1)
    sum1 = (sum1_w0, sum1_w1)

    def copy1(w, o):
        if w == 0:
            src, to = chip_w.at[w, :, lax.rem(y + o, s.ny)], at_y(o)
        else:
            src, to = chip_w.at[w, lax.rem(rec + o, s.nx)], at_x(o)
        return remote(src, recv1[w].at[o - 1], w1_send.at[w, o], w1_recv.at[w, o], to)

    def copy2(w, o):
        if w == 0:
            src, to = sum1[w].at[lax.rem(rec + o, s.nx)], at_x(o)
        else:
            src, to = sum1[w].at[lax.rem(y + o, s.ny)], at_y(o)
        return remote(src, recv2_w.at[w, o - 1], w2_send.at[w, o], w2_recv.at[w, o], to)

    def copy3(w, o):
        src = sum2_w.at[w, lax.rem(z + o, s.nz)]
        return remote(src, recv3_w.at[w, o - 1], w3_send.at[w, o], w3_recv.at[w, o], at_z(o))

    def copy4(w, o, back=False):
        held = full_w.at[w, lax.rem(rec + s.nx - o, s.nx) if back else rec]
        return remote(held, held, w4_send.at[w, o], w4_recv.at[w, o], at_x(o))

    n1 = (s.ny, s.nx)
    n2 = (s.nx, s.ny)

    def stage1(w):
        core_copy(w).wait_recv()

        def one(g, _):
            total = piece[w](g, core) + recv_w[w, g].astype(F32)
            total = total.astype(BF16)
            for i in range(s.nx):
                chip_w[w, i, lax.rem(g, s.ny), g // s.ny] = total[:, i * s.xw : (i + 1) * s.xw]
            return 0

        lax.fori_loop(0, pieces, one, 0)
        for o in range(1, n1[w]):
            copy1(w, o).start()

    def stage2(w):
        for o in range(1, n1[w]):
            copy1(w, o).wait_recv()

        def one(i, _):
            own = chip_w[w, i, y] if w == 0 else chip_w[w, rec, i]
            total = own.astype(F32)
            for o in range(1, n1[w]):
                total += recv1[w][o - 1, i].astype(F32)
            sum1[w][i] = total.astype(BF16)
            return 0

        lax.fori_loop(0, n2[w], one, 0)
        for o in range(1, n2[w]):
            copy2(w, o).start()

    def stage3(w):
        for o in range(1, n2[w]):
            copy2(w, o).wait_recv()
        total = (sum1[w][rec] if w == 0 else sum1[w][y]).astype(F32)
        for o in range(1, n2[w]):
            total += recv2_w[w, o - 1].astype(F32)
        sum2_w[w] = total.astype(BF16)
        for o in range(1, s.nz):
            copy3(w, o).start()

    scale = 1.0 / math.sqrt(s.recs * s.nx * t_len * tm_count)

    def stage4(w):
        for o in range(1, s.nz):
            copy3(w, o).wait_recv()
        total = sum2_w[w, z].astype(F32)
        for o in range(1, s.nz):
            total += recv3_w[w, o - 1].astype(F32)
        full_w[w, rec] = total * scale
        for o in range(1, s.nx):
            copy4(w, o).start()

    def stage5(w):
        for o in range(1, s.nx):
            copy4(w, o, True).wait_recv()
        block = jnp.concatenate([full_w[w, i] for i in range(s.nx)], axis=1)
        if w == 0:
            gwin_ref[:, 0:d] = block[0:8]
            gwin_ref[:, d : 2 * d] = block[8:16]
        else:
            gwout_ref[...] = block

    total = jnp.zeros((d, 2 * d), F32)
    for r in range(s.recs):
        total += lax.dot_general(convp_v[r], gx_v[r], tn, preferred_element_type=F32)
    w1_v[...] = total
    send_core(0)

    for r in range(s.recs):
        gx_time = lax.dot_general(order, gx_v[r], tn, preferred_element_type=F32).astype(BF16)
        grad = lax.dot_general(gx_time, win_v[...], nt, preferred_element_type=F32)
        grad += par_ref[7:8, :] * cot_v[r].astype(F32)
        head_v[r] = grad[0 : s.lag, :].astype(BF16)
        for l in range(4):
            ext_grad[r, l, 0:t_len, :] = grad[:, l * lw : (l + 1) * lw]
    grad_halo = remote(head_v, ghalo_v, halo_sem.at[2], halo_sem.at[3], at_tm(-1))
    grad_halo.start()

    entry = block_entry(0, fwd_scans, entering(0))

    def fwd_second(i, carry):
        state, sums = carry
        new = []
        s_re, s_im, s_gain = sums
        for r in range(s.recs):
            h_re, h_im = state[r]
            held = [None, None]
            for sub in (0, 1):
                j = 2 * i + sub
                k4 = wide(keep_v[r, rows(j), :])
                kh_re, kh_im = k4 * h_re, k4 * h_im
                d_re = e_v[r, rows(j), 0:d]
                d_im = e_v[r, rows(j), d : 2 * d]
                x_re = x_v[r, rows(j), 0:d]
                x_im = x_v[r, rows(j), d : 2 * d]
                s_re += d_re * kh_re + d_im * kh_im
                s_im += d_im * kh_re - d_re * kh_im
                s_gain += d_re * x_re + d_im * x_im
                m_re, m_im = mul(lr, li, kh_re, kh_im)
                h_re = m_re + gain * x_re
                h_im = m_im + gain * x_im
                held[sub] = (h_re, h_im)
            for part in range(2):
                hb_v[r, rows2(i), part * d : (part + 1) * d] = jnp.concatenate(
                    [held[0][part], held[1][part]], axis=0
                ).astype(BF16)
            new.append((h_re, h_im))
        return tuple(new), (s_re, s_im, s_gain)

    _, sums = lax.fori_loop(0, s.bl // 2, fwd_second, (tuple(entry), (zero, zero, zero)))
    for i, v in enumerate(sums):
        small_v[10 + i : 11 + i, :] = jnp.sum(v, axis=0, keepdims=True)
    small_v[13:16, :] = jnp.zeros((3, d), F32)

    total = jnp.zeros((2 * d, d), F32)
    for r in range(s.recs):
        total += lax.dot_general(hb_v[r], cotp_v[r], tn, preferred_element_type=F32)
    w2_v[...] = total
    send_core(1)
    stage1(0)

    for l in range(4):
        lanes = slice(l * lw, (l + 1) * lw)

        def tap_step(i, acc):
            r = i // per_rec
            base = pl.multiple_of(lax.rem(i, per_rec) * s.chunk, s.chunk)
            grad = ext_grad[r, l, pl.ds(base, s.chunk), :]
            return tuple(
                acc[k]
                + fold(grad * ext_act[r, l, pl.ds(base + s.lag - dil_ref[k], s.chunk), :])
                for k in range(TAPS)
            )

        acc = lax.fori_loop(
            0, s.recs * per_rec, tap_step, (jnp.zeros((8, lw), F32),) * TAPS
        )
        for k in range(TAPS):
            small_v[k : k + 1, lanes] = jnp.sum(acc[k], axis=0, keepdims=True)

    for c in range(s.core):
        for i in range(s.ny):
            lane = (c * (s.ny // 2) + i // 2) * s.sw
            ssend[c, i] = small_v[(i % 2) * 8 : (i % 2) * 8 + 8, lane : lane + s.sw]
    small_core = remote(ssend.at[other], srecv_core, sc_sem.at[0], sc_sem.at[1], at_core())
    small_core.start()

    stage1(1)

    def copy_sy(o):
        to = lax.rem(y + o, s.ny)
        return remote(ssum_core.at[to], srecv_y.at[o - 1], sy_send.at[o], sy_recv.at[o], at_y(o))

    def copy_sx(o, back=False):
        held = sx_v.at[lax.rem(rec + s.nx - o, s.nx) if back else rec]
        return remote(held, held, sx_send.at[o], sx_recv.at[o], at_x(o))

    def copy_sz(o, back=False):
        held = sz_v.at[lax.rem(z + s.nz - o, s.nz) if back else z]
        return remote(held, held, sz_send.at[o], sz_recv.at[o], at_z(o))

    def copy_sg(o, back=False):
        held = sall_v.at[core, lax.rem(y + s.ny - o, s.ny) if back else y]
        return remote(held, held, sg_send.at[o], sg_recv.at[o], at_y(o))

    def copy_sf(back=False):
        held = sall_v.at[other if back else core]
        return remote(held, held, sf_sem.at[0], sf_sem.at[1], at_core())

    small_core.wait_recv()
    ssum_core[...] = ssend[core] + srecv_core[...]
    for o in range(1, s.ny):
        copy_sy(o).start()

    stage2(0)

    for o in range(1, s.ny):
        copy_sy(o).wait_recv()
    total = ssum_core[y]
    for o in range(1, s.ny):
        total += srecv_y[o - 1]
    sx_v[rec] = total
    for o in range(1, s.nx):
        copy_sx(o).start()

    stage2(1)

    for o in range(1, s.nx):
        copy_sx(o, True).wait_recv()
    total = sx_v[0]
    for i in range(1, s.nx):
        total += sx_v[i]
    sz_v[z] = total
    for o in range(1, s.nz):
        copy_sz(o).start()

    stage3(0)

    grad_halo.wait_recv()
    for r in range(s.recs):
        for l in range(4):
            after = ghalo_v[r, :, l * lw : (l + 1) * lw].astype(F32)
            ext_grad[r, l, t_len : t_len + s.lag, :] = jnp.where(tm < tm_count - 1, after, 0.0)
    for l in range(4):
        lanes = slice(l * lw, (l + 1) * lw)
        taps_l = [convw_ref[k : k + 1, lanes] for k in range(TAPS)]

        def grad_step(i, _):
            r = i // per_rec
            base = pl.multiple_of(lax.rem(i, per_rec) * s.chunk, s.chunk)
            out = jnp.zeros((s.chunk, lw), F32)
            for k in range(TAPS):
                out += taps_l[k] * ext_grad[r, l, pl.ds(base + dil_ref[k], s.chunk), :]
            gin_ref[r, pl.ds(base, s.chunk), lanes] = out.astype(BF16)
            return 0

        lax.fori_loop(0, s.recs * per_rec, grad_step, 0)

    for o in range(1, s.nz):
        copy_sz(o, True).wait_recv()
    total = sz_v[0]
    for i in range(1, s.nz):
        total += sz_v[i]
    sall_v[core, y] = total
    for o in range(1, s.ny):
        copy_sg(o).start()

    stage3(1)
    stage4(0)

    for o in range(1, s.ny):
        copy_sg(o, True).wait_recv()
    copy_sf().start()

    stage4(1)

    copy_sf(True).wait_recv()

    def small_rows(which):
        return jnp.concatenate(
            [
                sall_v[lane // (s.ny // 2), 2 * (lane % (s.ny // 2)) + which]
                for lane in range(d // s.sw)
            ],
            axis=1,
        )

    low, high = small_rows(0), small_rows(1)
    taps_ref[0:8, :] = low * scale
    taps_ref[8:9, :] = high[0:1] * scale
    skip_ref[...] = high[1:2] * scale
    lam_g_re, lam_g_im, gain_g = high[2:3], high[3:4], high[4:5]
    radius_grad = lam_g_re * par_ref[3:4, :] + lam_g_im * par_ref[4:5, :]
    radius_grad = radius_grad - gain_g * par_ref[5:6, :]
    rate_ref[...] = -radius_grad * par_ref[6:7, :] * scale
    angle_ref[...] = (lam_g_im * lam_re - lam_g_re * lam_im) * scale

    stage5(0)
    stage5(1)

    act_halo.wait_send()
    grad_halo.wait_send()
    for way in range(2):
        for o in range(1, s.group):
            copy_a(way, o).wait_send()
        for o in range(1, s.nz):

            @pl.when(sends_b(way, o))
            def _():
                copy_b(way, o).wait_send()

    for w in range(2):
        core_copy(w).wait_send()
        for o in range(1, n1[w]):
            copy1(w, o).wait_send()
        for o in range(1, n2[w]):
            copy2(w, o).wait_send()
        for o in range(1, s.nz):
            copy3(w, o).wait_send()
        for o in range(1, s.nx):
            copy4(w, o).wait_send()
    small_core.wait_send()
    for o in range(1, s.ny):
        copy_sy(o).wait_send()
        copy_sg(o).wait_send()
    for o in range(1, s.nx):
        copy_sx(o).wait_send()
    for o in range(1, s.nz):
        copy_sz(o).wait_send()
    copy_sf().wait_send()


def on_device(
    lag,
    activations,
    cotangent,
    retain,
    dilation,
    conv_w,
    skip_gain,
    log_rate,
    mode_angle,
    w_in,
    w_out,
):
    recs, time_steps, features = activations.shape
    s = Sizes(lax.axis_size("tm"), lax.axis_size("rec"), time_steps, features, lag)
    d, t = s.d, s.t
    decay_rate = jnp.exp(log_rate)
    radius = jnp.exp(-decay_rate)
    cos, sin = jnp.cos(mode_angle), jnp.sin(mode_angle)
    in_gain = jnp.sqrt(-jnp.expm1(-2.0 * decay_rate))
    params = jnp.stack(
        [
            radius * cos,
            radius * sin,
            in_gain,
            cos,
            sin,
            radius / in_gain,
            radius * decay_rate,
            skip_gain,
        ]
    )
    vmem = pl.BlockSpec(memory_space=pltpu.VMEM)
    smem = pl.BlockSpec(memory_space=pltpu.SMEM)
    hbm = pl.BlockSpec(memory_space=pl.ANY)
    pieces = s.nz * s.ny
    dma = pltpu.SemaphoreType.DMA
    buffers = [
        ((recs, t, d), BF16),
        ((recs, t, d), BF16),
        ((d, 2 * d), BF16),
        ((2 * d, d), BF16),
        ((recs, lag, d), BF16),
        ((recs, 4, t + lag, s.lw), F32),
        ((recs, 4, t + lag, s.lw), F32),
        ((recs, t, d), BF16),
        ((recs, t, d), BF16),
        ((recs, t, d), BF16),
        ((recs, t, s.lw), F32),
        ((recs, t, 2 * d), F32),
        ((recs, t, 2 * d), F32),
        ((recs, t, 2 * d), BF16),
        ((recs, t, 2 * d), BF16),
        ((recs, lag, d), BF16),
        ((recs, lag, d), BF16),
        ((d, 2 * d), F32),
        ((2 * d, d), F32),
        ((2, s.group, 8, s.half + s.lw), F32),
        ((2, s.nz, 8, s.half + s.lw), F32),
        ((16, d), F32),
        ((s.core, s.ny, 8, s.sw), F32),
        ((s.ny, 8, s.sw), F32),
        ((s.ny, 8, s.sw), F32),
        ((s.ny - 1, 8, s.sw), F32),
        ((s.nx, 8, s.sw), F32),
        ((s.nz, 8, s.sw), F32),
        ((s.core, s.ny, 8, s.sw), F32),
        ((2, pieces, PIECE, d), BF16),
        ((2, pieces, PIECE, d), BF16),
        ((2, s.nx, s.ny, s.nz, PIECE, s.xw), BF16),
        ((s.ny - 1, s.nx, s.nz, PIECE, s.xw), BF16),
        ((s.nx - 1, s.ny, s.nz, PIECE, s.xw), BF16),
        ((s.nx, s.nz, PIECE, s.xw), BF16),
        ((s.ny, s.nz, PIECE, s.xw), BF16),
        ((2, max(s.nx, s.ny) - 1, s.nz, PIECE, s.xw), BF16),
        ((2, s.nz, PIECE, s.xw), BF16),
        ((2, s.nz - 1, PIECE, s.xw), BF16),
        ((2, s.nx, PIECE, s.xw), F32),
    ]
    most = max(s.nx, s.ny)
    semaphores = [
        (4,),
        (4,),
        (2, s.group),
        (2, s.group),
        (2, s.nz),
        (2, s.nz),
        (2, 2),
        (2, most),
        (2, most),
        (2, most),
        (2, most),
        (2, s.nz),
        (2, s.nz),
        (2, s.nx),
        (2, s.nx),
        (2,),
        (s.ny,),
        (s.ny,),
        (s.nx,),
        (s.nx,),
        (s.nz,),
        (s.nz,),
        (s.ny,),
        (s.ny,),
        (2,),
    ]
    out = pl.pallas_call(
        functools.partial(kernel, s),
        out_shape=(
            jax.ShapeDtypeStruct((recs, t, d), BF16),
            jax.ShapeDtypeStruct((TAPS, d), F32),
            jax.ShapeDtypeStruct((1, d), F32),
            jax.ShapeDtypeStruct((1, d), F32),
            jax.ShapeDtypeStruct((1, d), F32),
            jax.ShapeDtypeStruct((8, 2 * d), F32),
            jax.ShapeDtypeStruct((16, d), F32),
        ),
        in_specs=[smem, vmem, vmem, vmem, hbm, hbm, hbm, hbm],
        out_specs=(vmem,) * 7,
        scratch_shapes=[pltpu.VMEM(shape, dtype) for shape, dtype in buffers]
        + [dma(shape) for shape in semaphores],
        compiler_params=pltpu.CompilerParams(
            collective_id=0, has_side_effects=True, vmem_limit_bytes=56 * 1024 * 1024
        ),
        cost_estimate=pl.CostEstimate(
            flops=2 * 5 * recs * t * d * 2 * d, bytes_accessed=6 << 20, transcendentals=0
        ),
    )(dilation, retain, conv_w, params, activations, cotangent, w_in, w_out)
    grad_input, taps, skip, rate, angle, grad_w_in, grad_w_out = out
    return (
        grad_input,
        taps,
        skip.reshape(d),
        rate.reshape(d),
        angle.reshape(d),
        grad_w_in,
        grad_w_out,
    )


def build(mesh, lag):
    wide = P("rec", "tm", None)
    return jax.shard_map(
        functools.partial(on_device, lag),
        mesh=mesh,
        in_specs=(wide, wide, P("rec", "tm")) + (P(),) * 7,
        out_specs=(wide, P(), P(), P(), P(), P("tm", None), P("tm", None)),
        check_vma=False,
    )


def solution(mesh):
    return build(mesh, MAXLAG)
```

time: 1100 us -> 65.9 us (0.06); the launches traced: 1080 us -> 65.4 us
  blocking collectives: 693 us -> 0 us
  local copies, waits for them, and re-layouts: 165 us -> 8.56 us
  waiting for transfers between devices: 86 us -> 0 us
  other arithmetic: 76.2 us -> 0.02 us
  Pallas kernels: 0 us -> 56.2 us
  between operations: 44.7 us -> 0.68 us
    all_gather x8 -> x0, blocking collectives: 351 us -> none  [entering(): gathered = jax.tree.map(lambda a: lax.all_gather(a, axis), part)]
    unnamed x1 -> x0, blocking collectives: 265 us -> none
    psum x1 -> x0, waiting for transfers between devices: 86 us -> none  [on_device(): lax.psum(raw_w_in.astype(jnp.bfloat16), 'rec').astype(jnp.float32)]
    psum x1 -> x0, blocking collectives: 76.8 us -> none  [on_device(): lax.psum((raw_taps, raw_skip, lam_grad_re, lam_grad_im, gain_grad), ('tm'...]
    dynamic_slice x64 -> x0, local copies, waits for them, and re-layouts: 62.1 us -> none  [local_sweep(): lax.scan(advance, (zeros_state, zeros_state), (vals_re, vals_im, keep_til...]
    pallas_call x0 -> x1, Pallas kernels: none -> 56.2 us  [on_device(): pl.pallas_call(functools.partial(kernel, s), out_shape=(jax.ShapeDtypeStr...]
    slice x43 -> x0, local copies, waits for them, and re-layouts: 26.8 us -> none  [the longest x28 11.6 us: local_sweep(): lax.associative_scan(compose, block_elems, reverse=backward, axis=0)]
    add x138 -> x0, other arithmetic: 25.9 us -> none  [the longest x36 9.46 us: local_sweep(): lax.associative_scan(compose, block_elems, reverse=backward, axis=0)]
  transfers between devices with their start and end apart: 4 -> 0, of which waited for: 1 -> 0; matrix products, arithmetic and copies ran while one was open for 13% -> 0% of each run, Pallas kernels for 0% -> 0%
where the time goes in v1:
time: 65.9 us; the launch traced here: 65.4 us
  Pallas kernels  56.2 us (85%)
  local copies, waits for them, and re-layouts  8.56 us (13%)
  between operations  0.68 us (1%)
    pallas_call x1, Pallas kernels, on_device(): pl.pallas_call(functools.partial(kernel, s), out_shape=(jax.ShapeDtypeStr...  56.2 us
    unnamed x23, local copies, waits for them, and re-layouts  7.2 us

profile of v1, /device:TPU:1, one launch (start us, length us, event | category | flops | bytes accessed | tf_op | source)
XLA Modules:
  0.0 65.4 jit_solution(2283901310694062695)
XLA Ops:
  0.6 0.7 %fusion.4 = (f32[512]{0:T(512)S(1)}, f32[512]{0:T(512)S(1)}) fusion(f32[512]{0:T(512)} %param.17), kind=kLoop, calls=%fused_computation.6 | loop fusion | bytes 6144 | tf_op jit(solution)/shard_map/sin | solution.py:854
  1.4 0.0 copy-start.7
  1.4 0.7 %copy-done.7 = f32[512]{0:T(512)S(1)} copy-done((f32[512]{0:T(512)S(1)}, f32[512]{0:T(512)}, u32[]{:S(2)}) %copy-start.7) | copy-done | bytes 2072
  2.1 0.0 copy-start.3
  2.1 0.7 %copy-done.3 = f32[512]{0:T(512)S(1)} copy-done((f32[512]{0:T(512)S(1)}, f32[512]{0:T(512)}, u32[]{:S(2)}) %copy-start.3) | copy-done | bytes 2072
  2.8 0.6 stack.35.par_ref
  3.4 56.2 %shard_map.153 = (bf16[2,256,512]{2,1,0:T(8,128)(2,1)}, f32[9,512]{1,0:T(8,128)}, f32[1,512]{1,0:T(1,128)}, f32[1,512]{1,0:T(1,128)}, f32[1,512]{1,0:T(1,128)}, /*index=5*/f32[8,1024]{1,0:T(8,128)}, f32[16,512]{1,0:T(8,128)}) custom-call(s32[9]{0:T(128)} %dil_ref.1, f32[2,256]{1,0:T(2,128)} %retain_ref.1, f32[9,512]{1,0:T(8,128)} %convw_ref.1, ...), custom_call_target="tpu_custom_call" | custom-call | flops 2684354560 | bytes 6291456 | tf_op jit(solution)/shard_map/pallas_call | solution.py:943
  59.6 0.0 copy-start.2
  59.6 1.9 %copy.24 = bf16[2,256,512]{2,1,0:T(8,128)(2,1)} copy(bf16[2,256,512]{2,1,0:T(8,128)(2,1)} %get-tuple-element.35) | data formatting | bytes 1048576
  61.5 0.0 copy-done.2
  61.5 0.0 copy-start.6
  61.5 0.0 copy-start.1
  61.5 0.6 copy.25
  62.1 0.1 copy-done.6
  62.1 0.0 copy-start.5
  62.1 0.6 copy.26
  62.7 0.1 copy-done.5
  62.8 0.0 copy-start.4
  62.8 0.6 copy.27
  63.4 0.1 copy-done.4
  63.5 0.6 copy.28
  64.0 0.0 copy-done.1
  64.0 0.0 copy-start
  64.0 0.6 copy.29
  64.7 0.2 copy-done
  64.8 0.6 copy.30
  (1 shorter events, 0.0 us)
Async XLA Ops:
  1.4 0.7 %copy-start.7 = (f32[512]{0:T(512)S(1)}, f32[512]{0:T(512)}, u32[]{:S(2)}) copy-start(f32[512]{0:T(512)} %param.16) | copy-start | bytes 6148
  2.1 0.7 %copy-start.3 = (f32[512]{0:T(512)S(1)}, f32[512]{0:T(512)}, u32[]{:S(2)}) copy-start(f32[512]{0:T(512)} %param.15) | copy-start | bytes 6148
  59.6 1.9 %copy-start.2 = (f32[9,512]{1,0:T(8,128)S(1)}, f32[9,512]{1,0:T(8,128)}, u32[]{:S(2)}) copy-start(f32[9,512]{1,0:T(8,128)} %get-tuple-element.36) | copy-start | bytes 55300
  61.5 0.7 %copy-start.6 = (f32[1,512]{1,0:T(1,128)S(1)}, f32[1,512]{1,0:T(1,128)}, u32[]{:S(2)}) copy-start(f32[1,512]{1,0:T(1,128)} %get-tuple-element.16) | copy-start | bytes 6148
  61.5 2.6 %copy-start.1 = (f32[8,1024]{1,0:T(8,128)S(1)}, f32[8,1024]{1,0:T(8,128)}, u32[]{:S(2)}) copy-start(f32[8,1024]{1,0:T(8,128)} %get-tuple-element.40) | copy-start | bytes 98308
  62.1 0.7 %copy-start.5 = (f32[1,512]{1,0:T(1,128)S(1)}, f32[1,512]{1,0:T(1,128)}, u32[]{:S(2)}) copy-start(f32[1,512]{1,0:T(1,128)} %get-tuple-element.17) | copy-start | bytes 6148
  62.8 0.7 %copy-start.4 = (f32[1,512]{1,0:T(1,128)S(1)}, f32[1,512]{1,0:T(1,128)}, u32[]{:S(2)}) copy-start(f32[1,512]{1,0:T(1,128)} %get-tuple-element.18) | copy-start | bytes 6148
  64.0 0.8 %copy-start = (f32[16,512]{1,0:T(8,128)S(1)}, f32[16,512]{1,0:T(8,128)}, u32[]{:S(2)}) copy-start(f32[16,512]{1,0:T(8,128)} %get-tuple-element.41) | copy-start | bytes 98308

commit v2 on v1

v2 whole, which is shorter than its diff:
```python
import functools
import math

import jax
import jax.numpy as jnp
from jax import lax
from jax.experimental import pallas as pl
from jax.experimental.pallas import tpu as pltpu
from jax.sharding import PartitionSpec as P

TAPS = 9
MAXLAG = 128
NB = 8
PIECE = 16
F32 = jnp.float32
BF16 = jnp.bfloat16


class Sizes:
    def __init__(self, tm, rec, time_steps, features, lag):
        self.core = 2
        self.nx = rec
        self.ny = 4 if tm >= 64 else 2
        self.nz = tm // (self.core * self.ny)
        self.group = self.core * self.ny
        self.recs = 2
        self.t = time_steps
        self.d = features
        self.lag = lag
        self.bl = time_steps // NB
        self.lw = features // 4
        self.half = features // 2
        self.xw = features // rec
        self.sw = 2 * features // self.group
        self.chunk = min(64, lag)
        self.hz = self.nz // 2


def mul(ar, ai, br, bi):
    return ar * br - ai * bi, ar * bi + ai * br


def square_times(re, im, times):
    for _ in range(times):
        re, im = re * re - im * im, 2.0 * (re * im)
    return re, im


def one_minus_exp(u):
    series = jnp.ones_like(u)
    for n in range(12, 1, -1):
        series = 1.0 - u * (1.0 / n) * series
    return jnp.where(u < 1.0, u * series, 1.0 - jnp.exp(-u))


def log2(n):
    return n.bit_length() - 1


def kernel(
    s,
    dil_ref,
    retain_ref,
    convw_ref,
    skip_ref,
    rate_ref,
    angle_ref,
    act_hbm,
    cot_hbm,
    win_hbm,
    wout_hbm,
    gin_hbm,
    packed_ref,
    act_v,
    cot_v,
    win_v,
    wout_v,
    halo_v,
    ext_act,
    ext_grad,
    cotp_v,
    convb_v,
    convp_v,
    keep_v,
    e_v,
    x_v,
    hb_v,
    gx_v,
    head_v,
    ghalo_v,
    gin_v,
    w1_v,
    w2_v,
    scan_a,
    scan_b,
    small_v,
    skip_v,
    ssend,
    srecv,
    sx_v,
    sz_v,
    sall_v,
    send_w,
    recv_w,
    in_chip,
    in_recv1,
    in_sum1,
    in_recv2,
    in_sum2,
    in_recv3,
    in_full,
    out_chip,
    out_recv1,
    out_sum1,
    out_recv2,
    out_x,
    in_sem,
    halo_sem,
    ghalo_sem,
    gin_sem,
    a_send,
    a_recv,
    b_send,
    b_recv,
    wc_sem,
    i1_send,
    i1_recv,
    i2_send,
    i2_recv,
    i3_send,
    i3_recv,
    i4_send,
    i4_recv,
    o1_send,
    o1_recv,
    o2_send,
    o2_recv,
    o3_send,
    o3_recv,
    sr_send,
    sr_recv,
    sx_send,
    sx_recv,
    sz_send,
    sz_recv,
    sg_send,
    sg_recv,
):
    t_len, d, half, lw = s.t, s.d, s.half, s.lw
    tm = lax.axis_index("tm")
    rec = lax.axis_index("rec")
    core = lax.rem(tm, s.core)
    y = lax.rem(tm // s.core, s.ny)
    z = tm // s.group
    spot = lax.rem(tm, s.group)
    tm_count = s.nz * s.group
    other = 1 - core

    def at(tm_to, rec_to):
        return (tm_to, rec_to)

    def at_group(o):
        return at(z * s.group + lax.rem(spot + o, s.group), rec)

    def at_core():
        return at(tm + 1 - 2 * core, rec)

    def at_y(o):
        return at(z * s.group + lax.rem(y + o, s.ny) * s.core + core, rec)

    def at_z(o):
        return at(lax.rem(z + o, s.nz) * s.group + spot, rec)

    def at_x(o):
        return at(tm, lax.rem(rec + o, s.nx))

    def at_tm(o):
        return at(lax.rem(tm + o + tm_count, tm_count), rec)

    def remote(src, dst, ssem, rsem, to):
        return pltpu.make_async_remote_copy(
            src_ref=src,
            dst_ref=dst,
            send_sem=ssem,
            recv_sem=rsem,
            device_id=to,
            device_id_type=pl.DeviceIdType.MESH,
        )

    loads = [
        pltpu.make_async_copy(src, dst, in_sem.at[i])
        for i, (src, dst) in enumerate(
            ((cot_hbm, cot_v), (wout_hbm, wout_v), (act_hbm, act_v), (win_hbm, win_v))
        )
    ]
    barrier = pltpu.get_barrier_semaphore()
    partners = (
        [at_group(o) for o in range(1, s.group)]
        + [at_z(o) for o in range(1, s.nz)]
        + [at_x(o) for o in range(1, s.nx)]
        + [at_tm(1), at_tm(-1)]
    )
    for partner in partners:
        pl.semaphore_signal(
            barrier, inc=1, device_id=partner, device_id_type=pl.DeviceIdType.MESH
        )
    for load in loads:
        load.start()
    pl.semaphore_wait(barrier, len(partners))

    def act_halo(r):
        return remote(
            act_hbm.at[r, pl.ds(t_len - s.lag, s.lag), :],
            halo_v.at[r],
            halo_sem.at[r, 0],
            halo_sem.at[r, 1],
            at_tm(1),
        )

    for r in range(s.recs):
        act_halo(r).start()

    row = lax.broadcasted_iota(jnp.int32, (t_len, t_len), 0)
    col = lax.broadcasted_iota(jnp.int32, (t_len, t_len), 1)
    chosen = col == lax.rem(row, NB) * s.bl + row // NB
    order = jnp.where(chosen, 1.0, 0.0).astype(BF16)
    for r in range(s.recs):
        picked = jnp.sum(
            jnp.where(chosen, retain_ref[r : r + 1, :], 0.0), axis=1, keepdims=True
        )
        keep_v[r] = jnp.broadcast_to(picked, (t_len, lw))

    decay_rate = jnp.exp(rate_ref[...])
    radius = jnp.exp(-decay_rate)
    cos, sin = jnp.cos(angle_ref[...]), jnp.sin(angle_ref[...])
    lam_re = radius * cos
    lam_im = radius * sin
    in_gain = jnp.sqrt(one_minus_exp(2.0 * decay_rate))
    block_pow = [square_times(lam_re, lam_im, log2(s.bl))]
    for _ in range(2):
        block_pow.append(square_times(*block_pow[-1], 1))
    dev_pow = square_times(*block_pow[-1], 1)
    plane_pow = square_times(*dev_pow, log2(s.group))

    def packed(v):
        pair = jnp.concatenate([v[:, :half], v[:, half:]], axis=0)
        return jnp.concatenate([pair] * s.recs, axis=0)

    dev_pack = (packed(dev_pow[0]), packed(dev_pow[1]))
    plane_pack = (packed(plane_pow[0]), packed(plane_pow[1]))
    sub_row = lax.broadcasted_iota(jnp.int32, (NB, d), 0)
    sub_row_k = lax.broadcasted_iota(jnp.int32, (NB, lw), 0)

    def power_table(index):
        re = jnp.ones((NB, d), F32)
        im = jnp.zeros((NB, d), F32)
        for bit, (pr, pi) in zip((1, 2, 4), block_pow):
            nr, ni = mul(re, im, pr, pi)
            here = lax.rem(index // bit, 2) == 1
            re = jnp.where(here, nr, re)
            im = jnp.where(here, ni, im)
        return re, im

    def wide(k):
        return jnp.concatenate([k] * (d // k.shape[1]), axis=1)

    def block_scan(e_re, e_im, k, sign):
        for span, (pr, pi) in zip((1, 2, 4), block_pow):
            shift = span if sign > 0 else NB - span
            pi = sign * pi
            n_re = pltpu.roll(e_re, shift, 0)
            n_im = pltpu.roll(e_im, shift, 0)
            n_k = pltpu.roll(k, shift, 0)
            there = sub_row >= span if sign > 0 else sub_row < NB - span
            there_k = sub_row_k >= span if sign > 0 else sub_row_k < NB - span
            m_re, m_im = mul(pr, pi, n_re, n_im)
            k_wide = wide(k)
            e_re = e_re + jnp.where(there, k_wide * m_re, 0.0)
            e_im = e_im + jnp.where(there, k_wide * m_im, 0.0)
            k = jnp.where(there_k, k * n_k, k)
        return e_re, e_im, k

    def summarize(way, scans):
        last = NB - 1 if way == 0 else 0
        for r in range(s.recs):
            e_re, e_im, k = scans[r]
            for part, v in enumerate((e_re, e_im)):
                for h in range(2):
                    at_row = part * 4 + r * 2 + h
                    scan_a[way, spot, at_row : at_row + 1, 0:half] = v[
                        last : last + 1, h * half : (h + 1) * half
                    ]
                    scan_a[way, spot, at_row : at_row + 1, half : half + lw] = k[
                        last : last + 1, :
                    ]

    def copy_a(way, o, back=False):
        held = scan_a.at[way, lax.rem(spot + s.group - o, s.group) if back else spot]
        return remote(held, held, a_send.at[way, o], a_recv.at[way, o], at_group(o))

    def copy_b(way, o, back=False):
        held = scan_b.at[way, lax.rem(z + s.nz - o, s.nz) if back else z]
        return remote(held, held, b_send.at[way, o], b_recv.at[way, o], at_z(o))

    def sends_b(way, o):
        return z + o < s.nz if way == 0 else z + o >= s.nz

    def gets_b(way, o):
        return z - o >= 0 if way == 0 else z - o < 0

    def start_a(way):
        for o in range(1, s.group):
            copy_a(way, o).start()

    def advance(slot, state, pack, way):
        sign = 1.0 if way == 0 else -1.0
        k = slot[0:4, half : half + lw]
        k = jnp.concatenate([k] * (half // lw), axis=1)
        m_re, m_im = mul(pack[0], sign * pack[1], state[0], state[1])
        return slot[0:4, 0:half] + k * m_re, slot[4:8, 0:half] + k * m_im

    def in_order(count, way):
        return range(count) if way == 0 else range(count - 1, -1, -1)

    def plane_step(way):
        for o in range(1, s.group):
            copy_a(way, o, True).wait_recv()
        state = (jnp.zeros((4, half), F32), jnp.zeros((4, half), F32))
        k_all = jnp.ones((4, lw), F32)
        for i in in_order(s.group, way):
            slot = scan_a[way, i]
            state = advance(slot, state, dev_pack, way)
            k_all = k_all * slot[0:4, half : half + lw]
        scan_b[way, z, 0:4, 0:half] = state[0]
        scan_b[way, z, 4:8, 0:half] = state[1]
        scan_b[way, z, 0:4, half : half + lw] = k_all
        scan_b[way, z, 4:8, half : half + lw] = k_all
        for o in range(1, s.nz):

            @pl.when(sends_b(way, o))
            def _():
                copy_b(way, o).start()

    def entering(way):
        for o in range(1, s.nz):

            @pl.when(gets_b(way, o))
            def _():
                copy_b(way, o, True).wait_recv()

        state = (jnp.zeros((4, half), F32), jnp.zeros((4, half), F32))
        for i in in_order(s.nz, way):
            moved = advance(scan_b[way, i], state, plane_pack, way)
            use = i < z if way == 0 else i > z
            state = tuple(jnp.where(use, m, o) for m, o in zip(moved, state))
        for i in in_order(s.group, way):
            moved = advance(scan_a[way, i], state, dev_pack, way)
            use = i < spot if way == 0 else i > spot
            state = tuple(jnp.where(use, m, o) for m, o in zip(moved, state))
        return state

    def block_entry(way, scans, state):
        sign = 1.0 if way == 0 else -1.0
        index = sub_row if way == 0 else NB - 1 - sub_row
        pw_re, pw_im = power_table(index)
        pw_im = sign * pw_im
        shift = 1 if way == 0 else NB - 1
        out = []
        for r in range(s.recs):
            s_re, s_im = (
                jnp.concatenate([v[2 * r : 2 * r + 1], v[2 * r + 1 : 2 * r + 2]], axis=1)
                for v in state
            )
            e_re, e_im, k = scans[r]
            m_re, m_im = mul(pw_re, pw_im, s_re, s_im)
            k_wide = wide(pltpu.roll(k, shift, 0))
            first = index == 0
            out.append(
                (
                    jnp.where(first, s_re, pltpu.roll(e_re, shift, 0) + k_wide * m_re),
                    jnp.where(first, s_im, pltpu.roll(e_im, shift, 0) + k_wide * m_im),
                )
            )
        return out

    lr = jnp.broadcast_to(lam_re, (NB, d))
    li = jnp.broadcast_to(lam_im, (NB, d))
    gain = jnp.broadcast_to(in_gain, (NB, d))
    zero = jnp.zeros((NB, d), F32)

    def rows(j):
        return pl.ds(pl.multiple_of(j * NB, NB), NB)

    def rows2(i):
        return pl.ds(pl.multiple_of(i * 2 * NB, 2 * NB), 2 * NB)

    loads[0].wait()
    loads[1].wait()
    nt = (((1,), (1,)), ((), ()))
    tn = (((0,), (0,)), ((), ()))
    for r in range(s.recs):
        cotp_v[r] = jnp.dot(order, cot_v[r], preferred_element_type=F32).astype(BF16)
        e_v[r] = lax.dot_general(cotp_v[r], wout_v[...], nt, preferred_element_type=F32)

    def adj_first(i, carry):
        j = s.bl - 1 - i
        new = []
        for r in range(s.recs):
            p_re, p_im, k_all = carry[r]
            k = keep_v[r, rows(j), :]
            k4 = wide(k)
            d_re = e_v[r, rows(j), 0:d] + p_re
            d_im = e_v[r, rows(j), d : 2 * d] + p_im
            m_re, m_im = mul(lr, -li, d_re, d_im)
            new.append((k4 * m_re, k4 * m_im, k_all * k))
        return tuple(new)

    ones_k = jnp.ones((NB, lw), F32)
    ends = lax.fori_loop(0, s.bl, adj_first, ((zero, zero, ones_k),) * s.recs, unroll=4)
    keeps = [ends[r][2] for r in range(s.recs)]
    adj_scans = [block_scan(*ends[r], -1.0) for r in range(s.recs)]
    summarize(1, adj_scans)
    start_a(1)

    loads[2].wait()
    for r in range(s.recs):
        for l in range(4):
            ext_act[r, l, s.lag : s.lag + t_len, :] = act_v[
                r, :, l * lw : (l + 1) * lw
            ].astype(F32)
    per_rec = t_len // s.chunk

    def fold(v):
        return jnp.sum(v.reshape(s.chunk // 8, 8, lw), axis=0)

    def conv_block(l, r, base):
        lanes = slice(l * lw, (l + 1) * lw)
        base = pl.multiple_of(base, s.chunk)
        out = jnp.zeros((s.chunk, lw), F32)
        for k in range(TAPS):
            shifted = ext_act[r, l, pl.ds(base + s.lag - dil_ref[k], s.chunk), :]
            out += convw_ref[k : k + 1, lanes] * shifted
        convb_v[r, pl.ds(base, s.chunk), lanes] = out.astype(BF16)
        return fold(out * cot_v[r, pl.ds(base, s.chunk), lanes].astype(F32))

    low_chunks = s.lag // s.chunk
    high_chunks = per_rec - low_chunks
    none = jnp.zeros((8, lw), F32)
    for l in range(4):

        def high_step(i, acc):
            base = s.lag + lax.rem(i, high_chunks) * s.chunk
            return acc + conv_block(l, i // high_chunks, base)

        acc = lax.fori_loop(0, s.recs * high_chunks, high_step, none, unroll=2)
        skip_v[:, l * lw : (l + 1) * lw] = acc

    plane_step(1)

    loads[3].wait()
    for r in range(s.recs):
        act_halo(r).wait_recv()
        for l in range(4):
            lanes = slice(l * lw, (l + 1) * lw)
            before = halo_v[r, :, lanes].astype(F32)
            ext_act[r, l, 0 : s.lag, :] = jnp.where(tm > 0, before, 0.0)

            def low_step(i, acc):
                return acc + conv_block(l, r, i * s.chunk)

            skip_v[:, lanes] += lax.fori_loop(0, low_chunks, low_step, none, unroll=2)
        convp_v[r] = jnp.dot(order, convb_v[r], preferred_element_type=F32).astype(BF16)
        x_v[r] = jnp.dot(convp_v[r], win_v[...], preferred_element_type=F32)

    def fwd_first(j, carry):
        new = []
        for r in range(s.recs):
            h_re, h_im = carry[r]
            k4 = wide(keep_v[r, rows(j), :])
            m_re, m_im = mul(lr, li, h_re, h_im)
            new.append(
                (
                    k4 * m_re + x_v[r, rows(j), 0:d],
                    k4 * m_im + x_v[r, rows(j), d : 2 * d],
                )
            )
        return tuple(new)

    ends = lax.fori_loop(0, s.bl, fwd_first, ((zero, zero),) * s.recs, unroll=4)
    fwd_scans = [block_scan(*ends[r], keeps[r], 1.0) for r in range(s.recs)]
    summarize(0, fwd_scans)
    start_a(0)

    entry = block_entry(1, adj_scans, entering(1))

    def adj_second(i, carry):
        i = s.bl // 2 - 1 - i
        new = []
        for r in range(s.recs):
            p_re, p_im = carry[r]
            held = [None, None]
            for sub in (1, 0):
                j = 2 * i + sub
                k4 = wide(keep_v[r, rows(j), :])
                d_re = e_v[r, rows(j), 0:d] + p_re
                d_im = e_v[r, rows(j), d : 2 * d] + p_im
                e_v[r, rows(j), 0:d] = d_re
                e_v[r, rows(j), d : 2 * d] = d_im
                held[sub] = (gain * d_re, gain * d_im)
                m_re, m_im = mul(lr, -li, d_re, d_im)
                p_re, p_im = k4 * m_re, k4 * m_im
            for part in range(2):
                gx_v[r, rows2(i), part * d : (part + 1) * d] = jnp.concatenate(
                    [held[0][part], held[1][part]], axis=0
                ).astype(BF16)
            new.append((p_re, p_im))
        return tuple(new)

    lax.fori_loop(0, s.bl // 2, adj_second, tuple(entry), unroll=2)

    pieces = s.nz * s.ny
    part = pieces // 2

    def piece_in(g, c):
        at_row = pl.ds(pl.multiple_of((g * 2 + c) * 8, 8), 8)
        return jnp.concatenate([w1_v[at_row, 0:d], w1_v[at_row, d : 2 * d]], axis=0)

    def piece_out(g, c):
        return w2_v[pl.ds(pl.multiple_of((g * 2 + c) * PIECE, PIECE), PIECE), :]

    piece = (piece_in, piece_out)

    def core_copy(w, p):
        some = pl.ds(p * part, part)
        return remote(
            send_w.at[w, some],
            recv_w.at[w, some],
            wc_sem.at[w, p, 0],
            wc_sem.at[w, p, 1],
            at_core(),
        )

    def send_core(w, p):
        def one(g, _):
            send_w[w, g] = piece[w](g, other).astype(BF16)
            return 0

        lax.fori_loop(p * part, (p + 1) * part, one, 0, unroll=2)
        core_copy(w, p).start()

    def chip_sum(w, g):
        return (piece[w](g, core) + recv_w[w, g].astype(F32)).astype(BF16)

    def in_copy1(o):
        src = in_chip.at[lax.rem(rec + o, s.nx)]
        return remote(src, in_recv1.at[o - 1], i1_send.at[o], i1_recv.at[o], at_x(o))

    def in_copy2(o):
        src = in_sum1.at[lax.rem(y + o, s.ny)]
        return remote(src, in_recv2.at[o - 1], i2_send.at[o], i2_recv.at[o], at_y(o))

    def in_copy3(o):
        src = in_sum2.at[lax.rem(z + o, s.nz)]
        return remote(src, in_recv3.at[o - 1], i3_send.at[o], i3_recv.at[o], at_z(o))

    def in_copy4(o, back=False):
        held = in_full.at[lax.rem(rec + s.nx - o, s.nx) if back else rec]
        return remote(held, held, i4_send.at[o], i4_recv.at[o], at_x(o))

    def in_stage1():
        for p in range(2):
            core_copy(0, p).wait_recv()

        def one(g, _):
            total = chip_sum(0, g)
            for i in range(s.nx):
                in_chip[i, lax.rem(g, s.ny), g // s.ny] = total[:, i * s.xw : (i + 1) * s.xw]
            return 0

        lax.fori_loop(0, pieces, one, 0, unroll=4)
        for o in range(1, s.nx):
            in_copy1(o).start()

    def in_stage2():
        for o in range(1, s.nx):
            in_copy1(o).wait_recv()

        def one(i, _):
            total = in_chip[rec, i].astype(F32)
            for o in range(1, s.nx):
                total += in_recv1[o - 1, i].astype(F32)
            in_sum1[i] = total.astype(BF16)
            return 0

        lax.fori_loop(0, s.ny, one, 0)
        for o in range(1, s.ny):
            in_copy2(o).start()

    def in_stage3():
        for o in range(1, s.ny):
            in_copy2(o).wait_recv()
        total = in_sum1[y].astype(F32)
        for o in range(1, s.ny):
            total += in_recv2[o - 1].astype(F32)
        in_sum2[...] = total.astype(BF16)
        for o in range(1, s.nz):
            in_copy3(o).start()

    scale = 1.0 / math.sqrt(s.recs * s.nx * t_len * tm_count)

    def in_stage4():
        for o in range(1, s.nz):
            in_copy3(o).wait_recv()
        total = in_sum2[z].astype(F32)
        for o in range(1, s.nz):
            total += in_recv3[o - 1].astype(F32)
        in_full[rec] = total * scale
        for o in range(1, s.nx):
            in_copy4(o).start()

    def in_stage5():
        for o in range(1, s.nx):
            in_copy4(o, True).wait_recv()
        block = jnp.concatenate([in_full[i] for i in range(s.nx)], axis=1)
        packed_ref[16:32, :] = block

    def out_copy1(p, o):
        some = pl.ds(p * s.hz, s.hz)
        return remote(
            out_chip.at[lax.rem(y + o, s.ny), some],
            out_recv1.at[o - 1, some],
            o1_send.at[p, o],
            o1_recv.at[p, o],
            at_y(o),
        )

    def out_copy2(to):
        return remote(
            out_sum1.at[to],
            out_recv2.at[z],
            o2_send.at[to],
            o2_recv.at[z],
            at(to * s.group + spot, rec),
        )

    def out_from2(z_from):
        held = out_recv2.at[z_from]
        return remote(
            held, held, o2_send.at[z_from], o2_recv.at[z_from], at(z_from * s.group + spot, rec)
        )

    def out_copy3(o, back=False):
        held = out_x.at[lax.rem(rec + s.nx - o, s.nx) if back else rec]
        return remote(held, held, o3_send.at[o], o3_recv.at[o], at_x(o))

    def out_stage1(p):
        core_copy(1, p).wait_recv()

        def one(g, _):
            out_chip[lax.rem(g, s.ny), g // s.ny] = chip_sum(1, g)
            return 0

        lax.fori_loop(p * part, (p + 1) * part, one, 0, unroll=2)
        for o in range(1, s.ny):
            out_copy1(p, o).start()

    def out_stage2(p):
        for o in range(1, s.ny):
            out_copy1(p, o).wait_recv()
        for i in range(p * s.hz, (p + 1) * s.hz):
            total = out_chip[y, i].astype(F32)
            for o in range(1, s.ny):
                total += out_recv1[o - 1, i].astype(F32)
            out_sum1[i] = total.astype(BF16)

            @pl.when(i != z)
            def _():
                out_copy2(i).start()

    def out_stage3():
        for i in range(s.nz):

            @pl.when(i != z)
            def _():
                out_from2(i).wait_recv()

        out_recv2[z] = out_sum1[z]
        total = out_recv2[0].astype(F32)
        for i in range(1, s.nz):
            total += out_recv2[i].astype(F32)
        out_x[rec] = total.astype(BF16)
        for o in range(1, s.nx):
            out_copy3(o).start()

    def out_stage4():
        for o in range(1, s.nx):
            out_copy3(o, True).wait_recv()
        total = out_x[0].astype(F32)
        for i in range(1, s.nx):
            total += out_x[i].astype(F32)
        packed_ref[32:48, :] = total * scale

    half_d = d // 2
    for p in range(2):
        total = jnp.zeros((half_d, 2 * d), F32)
        for r in range(s.recs):
            total += lax.dot_general(
                convp_v[r, :, p * half_d : (p + 1) * half_d],
                gx_v[r],
                tn,
                preferred_element_type=F32,
            )
        w1_v[p * half_d : (p + 1) * half_d, :] = total
        send_core(0, p)

    plane_step(0)

    def grad_halo(r):
        return remote(
            head_v.at[r], ghalo_v.at[r], ghalo_sem.at[r, 0], ghalo_sem.at[r, 1], at_tm(-1)
        )

    for r in range(s.recs):
        gx_time = lax.dot_general(order, gx_v[r], tn, preferred_element_type=F32).astype(BF16)
        grad = lax.dot_general(gx_time, win_v[...], nt, preferred_element_type=F32)
        grad += skip_ref[...] * cot_v[r].astype(F32)
        head_v[r] = grad[0 : s.lag, :].astype(BF16)
        for l in range(4):
            ext_grad[r, l, 0:t_len, :] = grad[:, l * lw : (l + 1) * lw]
        grad_halo(r).start()

    in_stage1()

    for l in range(4):
        lanes = slice(l * lw, (l + 1) * lw)

        def tap_step(i, acc):
            r = i // per_rec
            base = pl.multiple_of(lax.rem(i, per_rec) * s.chunk, s.chunk)
            grad = ext_grad[r, l, pl.ds(base, s.chunk), :]
            return tuple(
                acc[k]
                + fold(grad * ext_act[r, l, pl.ds(base + s.lag - dil_ref[k], s.chunk), :])
                for k in range(TAPS)
            )

        acc = lax.fori_loop(0, s.recs * per_rec, tap_step, (none,) * TAPS, unroll=2)
        for k in range(TAPS):
            small_v[k : k + 1, lanes] = jnp.sum(acc[k], axis=0, keepdims=True)
    small_v[9:10, :] = jnp.sum(skip_v[...], axis=0, keepdims=True)

    entry = block_entry(0, fwd_scans, entering(0))

    def fwd_second(i, carry):
        state, sums = carry
        new = []
        s_re, s_im, s_gain = sums
        for r in range(s.recs):
            h_re, h_im = state[r]
            held = [None, None]
            for sub in (0, 1):
                j = 2 * i + sub
                k4 = wide(keep_v[r, rows(j), :])
                kh_re, kh_im = k4 * h_re, k4 * h_im
                d_re = e_v[r, rows(j), 0:d]
                d_im = e_v[r, rows(j), d : 2 * d]
                x_re = x_v[r, rows(j), 0:d]
                x_im = x_v[r, rows(j), d : 2 * d]
                s_re += d_re * kh_re + d_im * kh_im
                s_im += d_im * kh_re - d_re * kh_im
                s_gain += d_re * x_re + d_im * x_im
                m_re, m_im = mul(lr, li, kh_re, kh_im)
                h_re = m_re + x_re
                h_im = m_im + x_im
                held[sub] = (gain * h_re, gain * h_im)
            for part in range(2):
                hb_v[r, rows2(i), part * d : (part + 1) * d] = jnp.concatenate(
                    [held[0][part], held[1][part]], axis=0
                ).astype(BF16)
            new.append((h_re, h_im))
        return tuple(new), (s_re, s_im, s_gain)

    _, sums = lax.fori_loop(
        0, s.bl // 2, fwd_second, (tuple(entry), (zero, zero, zero)), unroll=2
    )
    for p in range(2):
        total = jnp.zeros((d, d), F32)
        for r in range(s.recs):
            total += lax.dot_general(
                hb_v[r, :, p * d : (p + 1) * d], cotp_v[r], tn, preferred_element_type=F32
            )
        w2_v[p * d : (p + 1) * d, :] = total
        send_core(1, p)

    sums = (in_gain * sums[0], in_gain * sums[1], sums[2])
    for i, v in enumerate(sums):
        small_v[10 + i : 11 + i, :] = jnp.sum(v, axis=0, keepdims=True)
    small_v[13:16, :] = jnp.zeros((3, d), F32)

    for i in range(s.group):
        lane = (i // 2) * s.sw
        ssend[i] = small_v[(i % 2) * 8 : (i % 2) * 8 + 8, lane : lane + s.sw]

    def copy_sr(o):
        src = ssend.at[lax.rem(spot + o, s.group)]
        return remote(src, srecv.at[o - 1], sr_send.at[o], sr_recv.at[o], at_group(o))

    def copy_sx(o, back=False):
        held = sx_v.at[lax.rem(rec + s.nx - o, s.nx) if back else rec]
        return remote(held, held, sx_send.at[o], sx_recv.at[o], at_x(o))

    def copy_sz(o, back=False):
        held = sz_v.at[lax.rem(z + s.nz - o, s.nz) if back else z]
        return remote(held, held, sz_send.at[o], sz_recv.at[o], at_z(o))

    def copy_sg(o, back=False):
        held = sall_v.at[lax.rem(spot + s.group - o, s.group) if back else spot]
        return remote(held, held, sg_send.at[o], sg_recv.at[o], at_group(o))

    for o in range(1, s.group):
        copy_sr(o).start()

    out_stage1(0)
    out_stage1(1)

    for o in range(1, s.group):
        copy_sr(o).wait_recv()
    total = ssend[spot]
    for o in range(1, s.group):
        total += srecv[o - 1]
    sx_v[rec] = total
    for o in range(1, s.nx):
        copy_sx(o).start()

    in_stage2()

    for r in range(s.recs):
        grad_halo(r).wait_recv()
        for l in range(4):
            after = ghalo_v[r, :, l * lw : (l + 1) * lw].astype(F32)
            ext_grad[r, l, t_len : t_len + s.lag, :] = jnp.where(tm < tm_count - 1, after, 0.0)
    for l in range(4):
        lanes = slice(l * lw, (l + 1) * lw)
        taps_l = [convw_ref[k : k + 1, lanes] for k in range(TAPS)]

        def grad_step(i, _):
            r = i // per_rec
            base = pl.multiple_of(lax.rem(i, per_rec) * s.chunk, s.chunk)
            out = jnp.zeros((s.chunk, lw), F32)
            for k in range(TAPS):
                out += taps_l[k] * ext_grad[r, l, pl.ds(base + dil_ref[k], s.chunk), :]
            gin_v[r, pl.ds(base, s.chunk), lanes] = out.astype(BF16)
            return 0

        lax.fori_loop(0, s.recs * per_rec, grad_step, 0, unroll=2)
    gin_copy = pltpu.make_async_copy(gin_v, gin_hbm, gin_sem)
    gin_copy.start()

    for o in range(1, s.nx):
        copy_sx(o, True).wait_recv()
    total = sx_v[0]
    for i in range(1, s.nx):
        total += sx_v[i]
    sz_v[z] = total
    for o in range(1, s.nz):
        copy_sz(o).start()

    out_stage2(0)
    in_stage3()

    for o in range(1, s.nz):
        copy_sz(o, True).wait_recv()
    total = sz_v[0]
    for i in range(1, s.nz):
        total += sz_v[i]
    sall_v[spot] = total
    for o in range(1, s.group):
        copy_sg(o).start()

    out_stage2(1)
    in_stage4()

    for o in range(1, s.group):
        copy_sg(o, True).wait_recv()

    def small_rows(which):
        return jnp.concatenate(
            [
                sall_v[2 * lane + which]
                for lane in range(d // s.sw)
            ],
            axis=1,
        )

    low, high = small_rows(0), small_rows(1)
    lam_g_re, lam_g_im, gain_g = high[2:3], high[3:4], high[4:5]
    radius_grad = lam_g_re * cos + lam_g_im * sin - gain_g * (radius / in_gain)
    packed_ref[0:8, :] = low * scale
    packed_ref[8:10, :] = high[0:2] * scale
    packed_ref[10:11, :] = -radius_grad * radius * decay_rate * scale
    packed_ref[11:12, :] = (lam_g_im * lam_re - lam_g_re * lam_im) * scale
    packed_ref[12:16, :] = jnp.zeros((4, d), F32)

    out_stage3()
    in_stage5()
    out_stage4()

    gin_copy.wait()
    for r in range(s.recs):
        act_halo(r).wait_send()
        grad_halo(r).wait_send()
    for way in range(2):
        for o in range(1, s.group):
            copy_a(way, o).wait_send()
        for o in range(1, s.nz):

            @pl.when(sends_b(way, o))
            def _():
                copy_b(way, o).wait_send()

    for w in range(2):
        for p in range(2):
            core_copy(w, p).wait_send()
    for o in range(1, s.group):
        copy_sr(o).wait_send()
        copy_sg(o).wait_send()
    for o in range(1, s.nx):
        in_copy1(o).wait_send()
        in_copy4(o).wait_send()
        out_copy3(o).wait_send()
        copy_sx(o).wait_send()
    for o in range(1, s.ny):
        in_copy2(o).wait_send()
        for p in range(2):
            out_copy1(p, o).wait_send()
    for o in range(1, s.nz):
        in_copy3(o).wait_send()
        copy_sz(o).wait_send()
    for i in range(s.nz):

        @pl.when(i != z)
        def _():
            out_copy2(i).wait_send()


def spread(gin_in, packed_ref, gin_out, taps_ref, skip_ref, rate_ref, angle_ref, win_ref, wout_ref):
    d = taps_ref.shape[1]
    gin_out[...] = gin_in[...]
    taps_ref[...] = packed_ref[0:TAPS, :]
    skip_ref[...] = packed_ref[9:10, :]
    rate_ref[...] = packed_ref[10:11, :]
    angle_ref[...] = packed_ref[11:12, :]
    win_ref[:, 0:d] = packed_ref[16:24, :]
    win_ref[:, d : 2 * d] = packed_ref[24:32, :]
    wout_ref[...] = packed_ref[32:48, :]


def on_device(
    lag,
    activations,
    cotangent,
    retain,
    dilation,
    conv_w,
    skip_gain,
    log_rate,
    mode_angle,
    w_in,
    w_out,
):
    recs, time_steps, features = activations.shape
    s = Sizes(lax.axis_size("tm"), lax.axis_size("rec"), time_steps, features, lag)
    d, t = s.d, s.t
    vmem = pl.BlockSpec(memory_space=pltpu.VMEM)
    smem = pl.BlockSpec(memory_space=pltpu.SMEM)
    hbm = pl.BlockSpec(memory_space=pl.ANY)
    pieces = s.nz * s.ny
    dma = pltpu.SemaphoreType.DMA
    buffers = [
        ((recs, t, d), BF16),
        ((recs, t, d), BF16),
        ((d, 2 * d), BF16),
        ((2 * d, d), BF16),
        ((recs, lag, d), BF16),
        ((recs, 4, t + lag, s.lw), F32),
        ((recs, 4, t + lag, s.lw), F32),
        ((recs, t, d), BF16),
        ((recs, t, d), BF16),
        ((recs, t, d), BF16),
        ((recs, t, s.lw), F32),
        ((recs, t, 2 * d), F32),
        ((recs, t, 2 * d), F32),
        ((recs, t, 2 * d), BF16),
        ((recs, t, 2 * d), BF16),
        ((recs, lag, d), BF16),
        ((recs, lag, d), BF16),
        ((recs, t, d), BF16),
        ((d, 2 * d), F32),
        ((2 * d, d), F32),
        ((2, s.group, 8, s.half + s.lw), F32),
        ((2, s.nz, 8, s.half + s.lw), F32),
        ((16, d), F32),
        ((8, d), F32),
        ((s.group, 8, s.sw), F32),
        ((s.group - 1, 8, s.sw), F32),
        ((s.nx, 8, s.sw), F32),
        ((s.nz, 8, s.sw), F32),
        ((s.group, 8, s.sw), F32),
        ((2, pieces, PIECE, d), BF16),
        ((2, pieces, PIECE, d), BF16),
        ((s.nx, s.ny, s.nz, PIECE, s.xw), BF16),
        ((s.nx - 1, s.ny, s.nz, PIECE, s.xw), BF16),
        ((s.ny, s.nz, PIECE, s.xw), BF16),
        ((s.ny - 1, s.nz, PIECE, s.xw), BF16),
        ((s.nz, PIECE, s.xw), BF16),
        ((s.nz - 1, PIECE, s.xw), BF16),
        ((s.nx, PIECE, s.xw), F32),
        ((s.ny, s.nz, PIECE, d), BF16),
        ((s.ny - 1, s.nz, PIECE, d), BF16),
        ((s.nz, PIECE, d), BF16),
        ((s.nz, PIECE, d), BF16),
        ((s.nx, PIECE, d), BF16),
    ]
    semaphores = [
        (4,),
        (recs, 2),
        (recs, 2),
        (),
        (2, s.group),
        (2, s.group),
        (2, s.nz),
        (2, s.nz),
        (2, 2, 2),
        (s.nx,),
        (s.nx,),
        (s.ny,),
        (s.ny,),
        (s.nz,),
        (s.nz,),
        (s.nx,),
        (s.nx,),
        (2, s.ny),
        (2, s.ny),
        (s.nz,),
        (s.nz,),
        (s.nx,),
        (s.nx,),
        (s.group,),
        (s.group,),
        (s.nx,),
        (s.nx,),
        (s.nz,),
        (s.nz,),
        (s.group,),
        (s.group,),
    ]
    gin, packed = pl.pallas_call(
        functools.partial(kernel, s),
        out_shape=(
            jax.ShapeDtypeStruct((recs, t, d), BF16),
            jax.ShapeDtypeStruct((48, d), F32),
        ),
        in_specs=[smem] + [vmem] * 5 + [hbm] * 4,
        out_specs=(hbm, vmem),
        scratch_shapes=[pltpu.VMEM(shape, dtype) for shape, dtype in buffers]
        + [dma if shape == () else dma(shape) for shape in semaphores],
        compiler_params=pltpu.CompilerParams(
            collective_id=0, has_side_effects=True, vmem_limit_bytes=56 * 1024 * 1024
        ),
        cost_estimate=pl.CostEstimate(
            flops=2 * 5 * recs * t * d * 2 * d, bytes_accessed=6 << 20, transcendentals=0
        ),
    )(
        dilation,
        retain,
        conv_w,
        skip_gain.reshape(1, d),
        log_rate.reshape(1, d),
        mode_angle.reshape(1, d),
        activations,
        cotangent,
        w_in,
        w_out,
    )
    grad_input, taps, skip, rate, angle, grad_w_in, grad_w_out = pl.pallas_call(
        spread,
        out_shape=(
            jax.ShapeDtypeStruct((recs, t, d), BF16),
            jax.ShapeDtypeStruct((TAPS, d), F32),
            jax.ShapeDtypeStruct((1, d), F32),
            jax.ShapeDtypeStruct((1, d), F32),
            jax.ShapeDtypeStruct((1, d), F32),
            jax.ShapeDtypeStruct((8, 2 * d), F32),
            jax.ShapeDtypeStruct((16, d), F32),
        ),
        in_specs=[vmem] * 2,
        out_specs=(vmem,) * 7,
    )(gin, packed)
    return (
        grad_input,
        taps,
        skip.reshape(d),
        rate.reshape(d),
        angle.reshape(d),
        grad_w_in,
        grad_w_out,
    )


def build(mesh, lag):
    wide = P("rec", "tm", None)
    return jax.shard_map(
        functools.partial(on_device, lag),
        mesh=mesh,
        in_specs=(wide, wide, P("rec", "tm")) + (P(),) * 7,
        out_specs=(wide, P(), P(), P(), P(), P("tm", None), P("tm", None)),
        check_vma=False,
    )


def solution(mesh):
    return build(mesh, MAXLAG)
```

time: 65.9 us -> 55.6 us (0.84)
  local copies, waits for them, and re-layouts: 8.56 us -> 0 us
  Pallas kernels: 56.2 us -> 54.8 us
    unnamed x23 -> x0, local copies, waits for them, and re-layouts: 7.2 us -> none
    pallas_call x1, Pallas kernels: 56.2 us -> 52.9 us  [on_device(): pl.pallas_call(functools.partial(kernel, s), out_shape=(jax.ShapeDtypeStr...]
    pallas_call x0 -> x1, Pallas kernels: none -> 1.89 us  [on_device(): pl.pallas_call(spread, out_shape=(jax.ShapeDtypeStruct((recs, t, d), BF16...]
    sin x1 -> x0, local copies, waits for them, and re-layouts: 0.72 us -> none  [on_device(): cos, sin = (jnp.cos(mode_angle), jnp.sin(mode_angle))]
where the time goes in v2:
time: 55.6 us; the launch traced here: 55.5 us
  Pallas kernels  54.8 us (99%)
  between operations  0.64 us (1%)
    pallas_call x1, Pallas kernels, on_device(): pl.pallas_call(functools.partial(kernel, s), out_shape=(jax.ShapeDtypeStr...  52.9 us
    pallas_call x1, Pallas kernels, on_device(): pl.pallas_call(spread, out_shape=(jax.ShapeDtypeStruct((recs, t, d), BF16...  1.89 us

profile of v2, /device:TPU:1, one launch (start us, length us, event | category | flops | bytes accessed | tf_op | source)
XLA Modules:
  0.0 55.5 jit_solution(374005158558181055)
XLA Ops:
  0.6 52.9 %shard_map.153 = (bf16[2,256,512]{2,1,0:T(8,128)(2,1)}, f32[48,512]{1,0:T(8,128)}) custom-call(s32[9]{0:T(128)} %dil_ref.1, f32[2,256]{1,0:T(2,128)} %retain_ref.1, f32[9,512]{1,0:T(8,128)} %convw_ref.1, f32[1,512]{1,0:T(1,128)} %bitcast.6, f32[1,512]{1,0:T(1,128)} %bitcast.7, f32[1,512]{1,0:T(1,128)} %bitcast.8, bf16[2,256,512]{2,1,0:T(8,128)(2,1)} %act_hbm.1, ...), custom_call_target="tpu_custom_call" | custom-call | flops 2684354560 | bytes 6291456 | tf_op jit(solution)/shard_map/pallas_call | solution.py:1057
  53.6 1.9 %shard_map.154 = (bf16[2,256,512]{2,1,0:T(8,128)(2,1)}, f32[9,512]{1,0:T(8,128)}, f32[1,512]{1,0:T(1,128)}, f32[1,512]{1,0:T(1,128)}, f32[1,512]{1,0:T(1,128)}, /*index=5*/f32[8,1024]{1,0:T(8,128)}, f32[16,512]{1,0:T(8,128)}) custom-call(bf16[2,256,512]{2,1,0:T(8,128)(2,1)} %get-tuple-element.16.gin_in, f32[48,512]{1,0:T(8,128)} %get-tuple-element.17.packed_ref), custom_call_target="tpu_custom_call" | custom-call | tf_op jit(solution)/shard_map/pallas_call | solution.py:1085

commit v3 on v2

--- a/solution.py
+++ b/solution.py
@@ -31,7 +31,7 @@
         self.lw = features // 4
         self.half = features // 2
         self.xw = features // rec
-        self.sw = 2 * features // self.group
+        self.sw = 2 * features // self.nz
         self.chunk = min(64, lag)
         self.hz = self.nz // 2
 
@@ -60,17 +60,22 @@
 def kernel(
     s,
     dil_ref,
-    retain_ref,
-    convw_ref,
-    skip_ref,
-    rate_ref,
-    angle_ref,
+    retain_hbm,
+    convw_hbm,
+    skip_hbm,
+    rate_hbm,
+    angle_hbm,
     act_hbm,
     cot_hbm,
     win_hbm,
     wout_hbm,
     gin_hbm,
     packed_ref,
+    retain_ref,
+    convw_ref,
+    skip_ref,
+    rate_ref,
+    angle_ref,
     act_v,
     cot_v,
     win_v,
@@ -89,8 +94,7 @@
     head_v,
     ghalo_v,
     gin_v,
-    w1_v,
-    w2_v,
+    gx_time_v,
     scan_a,
     scan_b,
     small_v,
@@ -98,9 +102,9 @@
     ssend,
     srecv,
     sx_v,
-    sz_v,
+    sp_v,
     sall_v,
-    send_w,
+    piece_v,
     recv_w,
     in_chip,
     in_recv1,
@@ -141,8 +145,8 @@
     sr_recv,
     sx_send,
     sx_recv,
-    sz_send,
-    sz_recv,
+    sp_send,
+    sp_recv,
     sg_send,
     sg_recv,
 ):
@@ -190,7 +194,17 @@
     loads = [
         pltpu.make_async_copy(src, dst, in_sem.at[i])
         for i, (src, dst) in enumerate(
-            ((cot_hbm, cot_v), (wout_hbm, wout_v), (act_hbm, act_v), (win_hbm, win_v))
+            (
+                (retain_hbm, retain_ref),
+                (rate_hbm, rate_ref),
+                (angle_hbm, angle_ref),
+                (cot_hbm, cot_v),
+                (wout_hbm, wout_v),
+                (act_hbm, act_v),
+                (convw_hbm, convw_ref),
+                (win_hbm, win_v),
+                (skip_hbm, skip_ref),
+            )
         )
     ]
     barrier = pltpu.get_barrier_semaphore()
@@ -224,6 +238,11 @@
     col = lax.broadcasted_iota(jnp.int32, (t_len, t_len), 1)
     chosen = col == lax.rem(row, NB) * s.bl + row // NB
     order = jnp.where(chosen, 1.0, 0.0).astype(BF16)
+    chosen_back = row == lax.rem(col, NB) * s.bl + col // NB
+    order_back = jnp.where(chosen_back, 1.0, 0.0).astype(BF16)
+    all_rows = s.recs * t_len
+    for i in range(3):
+        loads[i].wait()
     for r in range(s.recs):
         picked = jnp.sum(
             jnp.where(chosen, retain_ref[r : r + 1, :], 0.0), axis=1, keepdims=True
@@ -394,13 +413,15 @@
     def rows2(i):
         return pl.ds(pl.multiple_of(i * 2 * NB, 2 * NB), 2 * NB)
 
-    loads[0].wait()
-    loads[1].wait()
+    loads[3].wait()
+    loads[4].wait()
     nt = (((1,), (1,)), ((), ()))
     tn = (((0,), (0,)), ((), ()))
     for r in range(s.recs):
         cotp_v[r] = jnp.dot(order, cot_v[r], preferred_element_type=F32).astype(BF16)
-        e_v[r] = lax.dot_general(cotp_v[r], wout_v[...], nt, preferred_element_type=F32)
+    cot_rows = cotp_v[...].reshape(all_rows, d)
+    back = lax.dot_general(cot_rows, wout_v[...], nt, preferred_element_type=F32)
+    e_v[...] = back.reshape(s.recs, t_len, 2 * d)
 
     def adj_first(i, carry):
         j = s.bl - 1 - i
@@ -422,7 +443,8 @@
     summarize(1, adj_scans)
     start_a(1)
 
-    loads[2].wait()
+    loads[5].wait()
+    loads[6].wait()
     for r in range(s.recs):
         for l in range(4):
             ext_act[r, l, s.lag : s.lag + t_len, :] = act_v[
@@ -457,7 +479,8 @@
 
     plane_step(1)
 
-    loads[3].wait()
+    loads[7].wait()
+    loads[8].wait()
     for r in range(s.recs):
         act_halo(r).wait_recv()
         for l in range(4):
@@ -470,7 +493,10 @@
 
             skip_v[:, lanes] += lax.fori_loop(0, low_chunks, low_step, none, unroll=2)
         convp_v[r] = jnp.dot(order, convb_v[r], preferred_element_type=F32).astype(BF16)
-        x_v[r] = jnp.dot(convp_v[r], win_v[...], preferred_element_type=F32)
+    conv_rows = convp_v[...].reshape(all_rows, d)
+    x_v[...] = jnp.dot(conv_rows, win_v[...], preferred_element_type=F32).reshape(
+        s.recs, t_len, 2 * d
+    )
 
     def fwd_first(j, carry):
         new = []
@@ -521,47 +547,30 @@
     pieces = s.nz * s.ny
     part = pieces // 2
 
-    def piece_in(g, c):
-        at_row = pl.ds(pl.multiple_of((g * 2 + c) * 8, 8), 8)
-        return jnp.concatenate([w1_v[at_row, 0:d], w1_v[at_row, d : 2 * d]], axis=0)
-
-    def piece_out(g, c):
-        return w2_v[pl.ds(pl.multiple_of((g * 2 + c) * PIECE, PIECE), PIECE), :]
-
-    piece = (piece_in, piece_out)
-
     def core_copy(w, p):
         some = pl.ds(p * part, part)
         return remote(
-            send_w.at[w, some],
+            piece_v.at[w, some, other],
             recv_w.at[w, some],
             wc_sem.at[w, p, 0],
             wc_sem.at[w, p, 1],
             at_core(),
         )
 
-    def send_core(w, p):
-        def one(g, _):
-            send_w[w, g] = piece[w](g, other).astype(BF16)
-            return 0
-
-        lax.fori_loop(p * part, (p + 1) * part, one, 0, unroll=2)
-        core_copy(w, p).start()
-
     def chip_sum(w, g):
-        return (piece[w](g, core) + recv_w[w, g].astype(F32)).astype(BF16)
+        return (piece_v[w, g, core].astype(F32) + recv_w[w, g].astype(F32)).astype(BF16)
 
     def in_copy1(o):
         src = in_chip.at[lax.rem(rec + o, s.nx)]
         return remote(src, in_recv1.at[o - 1], i1_send.at[o], i1_recv.at[o], at_x(o))
 
     def in_copy2(o):
-        src = in_sum1.at[lax.rem(y + o, s.ny)]
-        return remote(src, in_recv2.at[o - 1], i2_send.at[o], i2_recv.at[o], at_y(o))
+        src = in_sum1.at[lax.rem(z + o, s.nz)]
+        return remote(src, in_recv2.at[o - 1], i2_send.at[o], i2_recv.at[o], at_z(o))
 
     def in_copy3(o):
-        src = in_sum2.at[lax.rem(z + o, s.nz)]
-        return remote(src, in_recv3.at[o - 1], i3_send.at[o], i3_recv.at[o], at_z(o))
+        src = in_sum2.at[lax.rem(y + o, s.ny)]
+        return remote(src, in_recv3.at[o - 1], i3_send.at[o], i3_recv.at[o], at_y(o))
 
     def in_copy4(o, back=False):
         held = in_full.at[lax.rem(rec + s.nx - o, s.nx) if back else rec]
@@ -574,7 +583,7 @@
         def one(g, _):
             total = chip_sum(0, g)
             for i in range(s.nx):
-                in_chip[i, lax.rem(g, s.ny), g // s.ny] = total[:, i * s.xw : (i + 1) * s.xw]
+                in_chip[i, g // s.ny, lax.rem(g, s.ny)] = total[:, i * s.xw : (i + 1) * s.xw]
             return 0
 
         lax.fori_loop(0, pieces, one, 0, unroll=4)
@@ -592,27 +601,27 @@
             in_sum1[i] = total.astype(BF16)
             return 0
 
-        lax.fori_loop(0, s.ny, one, 0)
-        for o in range(1, s.ny):
+        lax.fori_loop(0, s.nz, one, 0, unroll=2)
+        for o in range(1, s.nz):
             in_copy2(o).start()
 
     def in_stage3():
-        for o in range(1, s.ny):
+        for o in range(1, s.nz):
             in_copy2(o).wait_recv()
-        total = in_sum1[y].astype(F32)
-        for o in range(1, s.ny):
+        total = in_sum1[z].astype(F32)
+        for o in range(1, s.nz):
             total += in_recv2[o - 1].astype(F32)
         in_sum2[...] = total.astype(BF16)
-        for o in range(1, s.nz):
+        for o in range(1, s.ny):
             in_copy3(o).start()
 
     scale = 1.0 / math.sqrt(s.recs * s.nx * t_len * tm_count)
 
     def in_stage4():
-        for o in range(1, s.nz):
+        for o in range(1, s.ny):
             in_copy3(o).wait_recv()
-        total = in_sum2[z].astype(F32)
-        for o in range(1, s.nz):
+        total = in_sum2[y].astype(F32)
+        for o in range(1, s.ny):
             total += in_recv3[o - 1].astype(F32)
         in_full[rec] = total * scale
         for o in range(1, s.nx):
@@ -702,16 +711,15 @@
 
     half_d = d // 2
     for p in range(2):
-        total = jnp.zeros((half_d, 2 * d), F32)
-        for r in range(s.recs):
-            total += lax.dot_general(
-                convp_v[r, :, p * half_d : (p + 1) * half_d],
-                gx_v[r],
-                tn,
-                preferred_element_type=F32,
-            )
-        w1_v[p * half_d : (p + 1) * half_d, :] = total
-        send_core(0, p)
+        total = lax.dot_general(
+            convp_v[:, :, p * half_d : (p + 1) * half_d].reshape(all_rows, half_d),
+            gx_v[...].reshape(all_rows, 2 * d),
+            tn,
+            preferred_element_type=F32,
+        ).reshape(part, s.core, 8, 2 * d)
+        total = jnp.concatenate([total[..., 0:d], total[..., d : 2 * d]], axis=2)
+        piece_v[0, p * part : (p + 1) * part] = total.astype(BF16)
+        core_copy(0, p).start()
 
     plane_step(0)
 
@@ -721,8 +729,11 @@
         )
 
     for r in range(s.recs):
-        gx_time = lax.dot_general(order, gx_v[r], tn, preferred_element_type=F32).astype(BF16)
-        grad = lax.dot_general(gx_time, win_v[...], nt, preferred_element_type=F32)
+        gx_time_v[r] = jnp.dot(order_back, gx_v[r], preferred_element_type=F32).astype(BF16)
+    gx_rows = gx_time_v[...].reshape(all_rows, 2 * d)
+    grads = lax.dot_general(gx_rows, win_v[...], nt, preferred_element_type=F32)
+    for r in range(s.recs):
+        grad = grads[r * t_len : (r + 1) * t_len]
         grad += skip_ref[...] * cot_v[r].astype(F32)
         head_v[r] = grad[0 : s.lag, :].astype(BF16)
         for l in range(4):
@@ -784,53 +795,47 @@
         0, s.bl // 2, fwd_second, (tuple(entry), (zero, zero, zero)), unroll=2
     )
     for p in range(2):
-        total = jnp.zeros((d, d), F32)
-        for r in range(s.recs):
-            total += lax.dot_general(
-                hb_v[r, :, p * d : (p + 1) * d], cotp_v[r], tn, preferred_element_type=F32
-            )
-        w2_v[p * d : (p + 1) * d, :] = total
-        send_core(1, p)
+        total = lax.dot_general(
+            hb_v[:, :, p * d : (p + 1) * d].reshape(all_rows, d),
+            cotp_v[...].reshape(all_rows, d),
+            tn,
+            preferred_element_type=F32,
+        )
+        piece_v[1, p * part : (p + 1) * part] = total.astype(BF16).reshape(
+            part, s.core, PIECE, d
+        )
+        core_copy(1, p).start()
+
+    out_stage1(0)
+    out_stage1(1)
 
     sums = (in_gain * sums[0], in_gain * sums[1], sums[2])
     for i, v in enumerate(sums):
         small_v[10 + i : 11 + i, :] = jnp.sum(v, axis=0, keepdims=True)
     small_v[13:16, :] = jnp.zeros((3, d), F32)
 
-    for i in range(s.group):
+    for i in range(s.nz):
         lane = (i // 2) * s.sw
         ssend[i] = small_v[(i % 2) * 8 : (i % 2) * 8 + 8, lane : lane + s.sw]
 
     def copy_sr(o):
-        src = ssend.at[lax.rem(spot + o, s.group)]
-        return remote(src, srecv.at[o - 1], sr_send.at[o], sr_recv.at[o], at_group(o))
+        src = ssend.at[lax.rem(z + o, s.nz)]
+        return remote(src, srecv.at[o - 1], sr_send.at[o], sr_recv.at[o], at_z(o))
 
     def copy_sx(o, back=False):
         held = sx_v.at[lax.rem(rec + s.nx - o, s.nx) if back else rec]
         return remote(held, held, sx_send.at[o], sx_recv.at[o], at_x(o))
 
-    def copy_sz(o, back=False):
-        held = sz_v.at[lax.rem(z + s.nz - o, s.nz) if back else z]
-        return remote(held, held, sz_send.at[o], sz_recv.at[o], at_z(o))
+    def copy_sp(o, back=False):
+        held = sp_v.at[lax.rem(spot + s.group - o, s.group) if back else spot]
+        return remote(held, held, sp_send.at[o], sp_recv.at[o], at_group(o))
 
     def copy_sg(o, back=False):
-        held = sall_v.at[lax.rem(spot + s.group - o, s.group) if back else spot]
-        return remote(held, held, sg_send.at[o], sg_recv.at[o], at_group(o))
-
-    for o in range(1, s.group):
+        held = sall_v.at[lax.rem(z + s.nz - o, s.nz) if back else z]
+        return remote(held, held, sg_send.at[o], sg_recv.at[o], at_z(o))
+
+    for o in range(1, s.nz):
         copy_sr(o).start()
-
-    out_stage1(0)
-    out_stage1(1)
-
-    for o in range(1, s.group):
-        copy_sr(o).wait_recv()
-    total = ssend[spot]
-    for o in range(1, s.group):
-        total += srecv[o - 1]
-    sx_v[rec] = total
-    for o in range(1, s.nx):
-        copy_sx(o).start()
 
     in_stage2()
 
@@ -856,31 +861,43 @@
     gin_copy = pltpu.make_async_copy(gin_v, gin_hbm, gin_sem)
     gin_copy.start()
 
+    for o in range(1, s.nz):
+        copy_sr(o).wait_recv()
+    total = ssend[z]
+    for o in range(1, s.nz):
+        total += srecv[o - 1]
+    sx_v[rec] = total
+    for o in range(1, s.nx):
+        copy_sx(o).start()
+
+    out_stage2(0)
+
     for o in range(1, s.nx):
         copy_sx(o, True).wait_recv()
     total = sx_v[0]
     for i in range(1, s.nx):
         total += sx_v[i]
-    sz_v[z] = total
+    sp_v[spot] = total
+    for o in range(1, s.group):
+        copy_sp(o).start()
+
+    out_stage2(1)
+
+    in_stage3()
+
+    for o in range(1, s.group):
+        copy_sp(o, True).wait_recv()
+    total = sp_v[0]
+    for i in range(1, s.group):
+        total += sp_v[i]
+    sall_v[z] = total
     for o in range(1, s.nz):
-        copy_sz(o).start()
-
-    out_stage2(0)
-    in_stage3()
+        copy_sg(o).start()
+
+    out_stage3()
+    in_stage4()
 
     for o in range(1, s.nz):
-        copy_sz(o, True).wait_recv()
-    total = sz_v[0]
-    for i in range(1, s.nz):
-        total += sz_v[i]
-    sall_v[spot] = total
-    for o in range(1, s.group):
-        copy_sg(o).start()
-
-    out_stage2(1)
-    in_stage4()
-
-    for o in range(1, s.group):
         copy_sg(o, True).wait_recv()
 
     def small_rows(which):
@@ -901,11 +918,6 @@
     packed_ref[11:12, :] = (lam_g_im * lam_re - lam_g_re * lam_im) * scale
     packed_ref[12:16, :] = jnp.zeros((4, d), F32)
 
-    out_stage3()
-    in_stage5()
-    out_stage4()
-
-    gin_copy.wait()
     for r in range(s.recs):
         act_halo(r).wait_send()
         grad_halo(r).wait_send()
@@ -922,20 +934,28 @@
         for p in range(2):
             core_copy(w, p).wait_send()
     for o in range(1, s.group):
-        copy_sr(o).wait_send()
-        copy_sg(o).wait_send()
+        copy_sp(o).wait_send()
     for o in range(1, s.nx):
         in_copy1(o).wait_send()
-        in_copy4(o).wait_send()
-        out_copy3(o).wait_send()
         copy_sx(o).wait_send()
     for o in range(1, s.ny):
-        in_copy2(o).wait_send()
         for p in range(2):
             out_copy1(p, o).wait_send()
     for o in range(1, s.nz):
+        in_copy2(o).wait_send()
+        copy_sr(o).wait_send()
+
+    in_stage5()
+    out_stage4()
+
+    gin_copy.wait()
+    for o in range(1, s.nz):
+        copy_sg(o).wait_send()
+    for o in range(1, s.nx):
+        in_copy4(o).wait_send()
+        out_copy3(o).wait_send()
+    for o in range(1, s.ny):
         in_copy3(o).wait_send()
-        copy_sz(o).wait_send()
     for i in range(s.nz):
 
         @pl.when(i != z)
@@ -977,6 +997,11 @@
     pieces = s.nz * s.ny
     dma = pltpu.SemaphoreType.DMA
     buffers = [
+        ((recs, t), F32),
+        ((TAPS, d), F32),
+        ((1, d), F32),
+        ((1, d), F32),
+        ((1, d), F32),
         ((recs, t, d), BF16),
         ((recs, t, d), BF16),
         ((d, 2 * d), BF16),
@@ -995,25 +1020,24 @@
         ((recs, lag, d), BF16),
         ((recs, lag, d), BF16),
         ((recs, t, d), BF16),
-        ((d, 2 * d), F32),
-        ((2 * d, d), F32),
+        ((recs, t, 2 * d), BF16),
         ((2, s.group, 8, s.half + s.lw), F32),
         ((2, s.nz, 8, s.half + s.lw), F32),
         ((16, d), F32),
         ((8, d), F32),
+        ((s.nz, 8, s.sw), F32),
+        ((s.nz - 1, 8, s.sw), F32),
+        ((s.nx, 8, s.sw), F32),
         ((s.group, 8, s.sw), F32),
-        ((s.group - 1, 8, s.sw), F32),
-        ((s.nx, 8, s.sw), F32),
         ((s.nz, 8, s.sw), F32),
-        ((s.group, 8, s.sw), F32),
+        ((2, pieces, s.core, PIECE, d), BF16),
         ((2, pieces, PIECE, d), BF16),
-        ((2, pieces, PIECE, d), BF16),
-        ((s.nx, s.ny, s.nz, PIECE, s.xw), BF16),
-        ((s.nx - 1, s.ny, s.nz, PIECE, s.xw), BF16),
-        ((s.ny, s.nz, PIECE, s.xw), BF16),
-        ((s.ny - 1, s.nz, PIECE, s.xw), BF16),
-        ((s.nz, PIECE, s.xw), BF16),
-        ((s.nz - 1, PIECE, s.xw), BF16),
+        ((s.nx, s.nz, s.ny, PIECE, s.xw), BF16),
+        ((s.nx - 1, s.nz, s.ny, PIECE, s.xw), BF16),
+        ((s.nz, s.ny, PIECE, s.xw), BF16),
+        ((s.nz - 1, s.ny, PIECE, s.xw), BF16),
+        ((s.ny, PIECE, s.xw), BF16),
+        ((s.ny - 1, PIECE, s.xw), BF16),
         ((s.nx, PIECE, s.xw), F32),
         ((s.ny, s.nz, PIECE, d), BF16),
         ((s.ny - 1, s.nz, PIECE, d), BF16),
@@ -1022,7 +1046,7 @@
         ((s.nx, PIECE, d), BF16),
     ]
     semaphores = [
-        (4,),
+        (9,),
         (recs, 2),
         (recs, 2),
         (),
@@ -1033,10 +1057,10 @@
         (2, 2, 2),
         (s.nx,),
         (s.nx,),
+        (s.nz,),
+        (s.nz,),
         (s.ny,),
         (s.ny,),
-        (s.nz,),
-        (s.nz,),
         (s.nx,),
         (s.nx,),
         (2, s.ny),
@@ -1045,14 +1069,14 @@
         (s.nz,),
         (s.nx,),
         (s.nx,),
+        (s.nz,),
+        (s.nz,),
+        (s.nx,),
+        (s.nx,),
         (s.group,),
         (s.group,),
-        (s.nx,),
-        (s.nx,),
         (s.nz,),
         (s.nz,),
-        (s.group,),
-        (s.group,),
     ]
     gin, packed = pl.pallas_call(
         functools.partial(kernel, s),
@@ -1060,7 +1084,7 @@
             jax.ShapeDtypeStruct((recs, t, d), BF16),
             jax.ShapeDtypeStruct((48, d), F32),
         ),
-        in_specs=[smem] + [vmem] * 5 + [hbm] * 4,
+        in_specs=[smem] + [hbm] * 9,
         out_specs=(hbm, vmem),
         scratch_shapes=[pltpu.VMEM(shape, dtype) for shape, dtype in buffers]
         + [dma if shape == () else dma(shape) for shape in semaphores],

time: 55.6 us -> 53.1 us (0.955)
  Pallas kernels: 54.8 us -> 52.4 us
    pallas_call x1, Pallas kernels: 52.9 us -> 50.5 us  [on_device(): pl.pallas_call(functools.partial(kernel, s), out_shape=(jax.ShapeDtypeStr...]
where the time goes in v3:
time: 53.1 us; the launch traced here: 53 us
  Pallas kernels  52.4 us (99%)
  between operations  0.64 us (1%)
    pallas_call x1, Pallas kernels, on_device(): pl.pallas_call(functools.partial(kernel, s), out_shape=(jax.ShapeDtypeStr...  50.5 us
    pallas_call x1, Pallas kernels, on_device(): pl.pallas_call(spread, out_shape=(jax.ShapeDtypeStruct((recs, t, d), BF16...  1.89 us

profile of v3, /device:TPU:1, one launch (start us, length us, event | category | flops | bytes accessed | tf_op | source)
XLA Modules:
  0.0 53.0 jit_solution(3238272144069886562)
XLA Ops:
  0.6 50.5 %shard_map.153 = (bf16[2,256,512]{2,1,0:T(8,128)(2,1)}, f32[48,512]{1,0:T(8,128)}) custom-call(s32[9]{0:T(128)} %dil_ref.1, f32[2,256]{1,0:T(2,128)} %retain_hbm.1, f32[9,512]{1,0:T(8,128)} %convw_hbm.1, f32[1,512]{1,0:T(1,128)} %bitcast.6, f32[1,512]{1,0:T(1,128)} %bitcast.7, f32[1,512]{1,0:T(1,128)} %bitcast.8, bf16[2,256,512]{2,1,0:T(8,128)(2,1)} %act_hbm.1, ...), custom_call_target="tpu_custom_call" | custom-call | flops 2684354560 | bytes 6291456 | tf_op jit(solution)/shard_map/pallas_call | solution.py:1081
  51.1 1.9 %shard_map.154 = (bf16[2,256,512]{2,1,0:T(8,128)(2,1)}, f32[9,512]{1,0:T(8,128)}, f32[1,512]{1,0:T(1,128)}, f32[1,512]{1,0:T(1,128)}, f32[1,512]{1,0:T(1,128)}, /*index=5*/f32[8,1024]{1,0:T(8,128)}, f32[16,512]{1,0:T(8,128)}) custom-call(bf16[2,256,512]{2,1,0:T(8,128)(2,1)} %get-tuple-element.16.gin_in, f32[48,512]{1,0:T(8,128)} %get-tuple-element.17.packed_ref), custom_call_target="tpu_custom_call" | custom-call | tf_op jit(solution)/shard_map/pallas_call | solution.py:1109
